TPU v7x, 32 devices: a whole 2x2x4 slice. The times are simulated.
32 devices in a mesh: dp: 8 (over z, x), mp: 4 (over y, core).
Axes of the slice: x: 2, y: 2, z: 4, core: 2. Of those that a mesh axis runs over, the one named last changes fastest.
Arguments:
- frames: bfloat16 [128, 30, 4, 84, 84], P(('dp', 'mp')), may hold values from 0 to 1
- returns: float32 [128, 30], P(('dp', 'mp')), may hold values from 0 to 4
- actions: int32 [128, 30], P(('dp', 'mp')), may hold values from 0 to 17
- starts: int32 [128], P(('dp', 'mp')), may hold values from 0 to 4066
- lengths: int32 [128], P(('dp', 'mp')), may hold values from 1 to 30, as said below
- shared_weights: float32 [1010688], replicated
- shared_first: float32 [1010688], replicated, may hold values from -0.00012207031 to 0.00012207031
- shared_second: float32 [1010688], replicated, may hold values from 3.5589012e-10 to 1.4235605e-09
- split_weights: float32 [394240], P('mp')
- split_first: float32 [394240], P('mp'), may hold values from -0.00012207031 to 0.00012207031
- split_second: float32 [394240], P('mp'), may hold values from 3.5589012e-10 to 1.4235605e-09
Outputs:
- shared_new: float32 [1010688], replicated
- shared_first_new: float32 [1010688], replicated
- shared_second_new: float32 [1010688], replicated
- shared_low: bfloat16 [1010688], replicated
- split_new: float32 [394240], P('mp')
- split_first_new: float32 [394240], P('mp')
- split_second_new: float32 [394240], P('mp')
- split_low: bfloat16 [394240], P('mp')
- grad_norm: float32 [], replicated
- loss_sum: float32 [], replicated
- valid_count: float32 [], replicated
Inputs may be any that keep to these rules, and one draw needn't show every extreme that they name: `lengths`: lengths are heavy-tailed and larger on later windows; the last window of all has 30.
All inputs are finite; a program needn't handle non-finite values.
Results may differ from a plain program's by a relative error of at most 0.001.
Values sent between devices are 32-bit elements; how exact they have to be, the bound alone decides.
A program may use at most 192 MiB of HBM per device.

v0:
```python
from functools import partial
import math

import jax
import jax.numpy as jnp
from jax import lax
from jax.sharding import PartitionSpec as P

D = 128
FF = 512
ACT = 18
C1 = 32
C2 = 64
TSTEPS = 4096
LAYERS = 2
STEP = 10
HD = 16


highest = lax.Precision.HIGHEST
clip_limit = 0.1
learn_rate = 0.05
beta_first = 0.9
beta_second = 0.95
adam_epsilon = 1e-08
weight_decay = 0.1


def shared_layout():
    return [
        ("conv_one", (C1, 4, 8, 8)),
        ("bias_one", (C1,)),
        ("conv_two", (C2, C1, 4, 4)),
        ("bias_two", (C2,)),
        ("conv_three", (C2, C2, 3, 3)),
        ("bias_three", (C2,)),
        ("encoder", (49 * C2, D)),
        ("vectors", (6 * LAYERS + 5, D)),
        ("action_table", (ACT, D)),
        ("time_table", (TSTEPS, D)),
        ("head", (D, ACT)),
    ]


def unpack_shared(flat):
    params = {}
    offset = 0
    for name, shape in shared_layout():
        count = math.prod(shape)
        params[name] = flat[offset : offset + count].reshape(shape)
        offset += count
    return params


def pack_shared(grads, total):
    flat = jnp.concatenate([grads[name].reshape(-1) for name, shape in shared_layout()])
    return jnp.concatenate([flat, jnp.zeros((total - flat.shape[0],), jnp.float32)])


def span_layout(narrow, hidden):
    return [
        ("qkv", (D, 3, narrow)),
        ("output", (narrow, D)),
        ("up", (D, hidden)),
        ("up_bias", (hidden,)),
        ("down", (hidden, D)),
    ]


def assemble(flat, copies, narrow, hidden):
    layout = span_layout(narrow, hidden)
    width = sum((math.prod(shape) for name, shape in layout))
    blocks = flat.reshape(copies, LAYERS, width)
    layers = []
    for layer in range(LAYERS):
        offset = 0
        pieces = {}
        for name, shape in layout:
            count = math.prod(shape)
            pieces[name] = blocks[:, layer, offset : offset + count].reshape((copies,) + shape)
            offset += count
        layers.append(
            {
                "qkv": jnp.moveaxis(pieces["qkv"], 0, 2).reshape(D, 3, copies * narrow),
                "output": pieces["output"].reshape(copies * narrow, D),
                "up": jnp.moveaxis(pieces["up"], 0, 1).reshape(D, copies * hidden),
                "up_bias": pieces["up_bias"].reshape(copies * hidden),
                "down": pieces["down"].reshape(copies * hidden, D),
            }
        )
    return layers


def conv_layer(images, kernel, bias, stride):
    result = lax.conv_general_dilated(
        images,
        kernel,
        (stride, stride),
        "VALID",
        dimension_numbers=("NCHW", "OIHW", "NCHW"),
        precision=highest,
    )
    return jax.nn.gelu(result + bias[None, :, None, None])


def embed_tokens(params, frames, returns, actions, starts):
    wins, steps = returns.shape
    images = frames.reshape(wins * steps, 4, 84, 84)
    hidden = conv_layer(images, params["conv_one"], params["bias_one"], 4)
    hidden = conv_layer(hidden, params["conv_two"], params["bias_two"], 2)
    hidden = conv_layer(hidden, params["conv_three"], params["bias_three"], 1)
    rows = params["vectors"]
    base = 6 * LAYERS
    states = jnp.tanh(
        jnp.dot(hidden.reshape(wins * steps, -1), params["encoder"], precision=highest)
        + rows[base + 4]
    )
    states = states.reshape(wins, steps, D)
    rewards = jnp.tanh(returns[:, :, None] * rows[base + 2] + rows[base + 3])
    picks = jax.nn.one_hot(actions, ACT, dtype=jnp.float32)
    moves = jnp.tanh(jnp.einsum("wsa,ad->wsd", picks, params["action_table"], precision=highest))
    places = starts[:, None] + jnp.arange(steps, dtype=jnp.int32)[None, :]
    times = jnp.take(params["time_table"], places, axis=0)
    tokens = jnp.stack([rewards, states, moves], axis=2) + times[:, :, None, :]
    return tokens.reshape(wins * 3 * steps, D)


def layer_norm(stream, gain, bias):
    centered = stream - jnp.mean(stream, -1, keepdims=True)
    spread = jnp.mean(centered * centered, -1, keepdims=True)
    return centered * lax.rsqrt(spread + 1e-05) * gain + bias


def attention(normed, qkv, output, lengths):
    wins = lengths.shape[0]
    tokens = normed.shape[0] // wins
    heads = qkv.shape[-1] // HD
    mixed = jnp.dot(normed, qkv.reshape(D, -1), precision=highest).reshape(
        wins, tokens, 3, heads, HD
    )
    query, keys, values = (mixed[:, :, 0], mixed[:, :, 1], mixed[:, :, 2])
    scores = jnp.einsum("wqhe,wkhe->whqk", query, keys, precision=highest) * HD ** (-0.5)
    place = jnp.arange(tokens, dtype=jnp.int32)
    allowed = (place[None, :, None] >= place[None, None, :]) & (
        place[None, None, :] < 3 * lengths[:, None, None]
    )
    scores = jnp.where(allowed[:, None], scores, -1e30)
    peak = jnp.max(scores, -1, keepdims=True)
    weights = jnp.exp(scores - peak)
    weights = weights / jnp.sum(weights, -1, keepdims=True)
    context = jnp.einsum("whqk,wkhe->wqhe", weights, values, precision=highest).reshape(
        wins * tokens, heads * HD
    )
    return jnp.dot(context, output, precision=highest)


def feed_forward(normed, up, up_bias, down):
    inner = jax.nn.gelu(jnp.dot(normed, up, precision=highest) + up_bias)
    return jnp.dot(inner, down, precision=highest)


def first_piece(stream, vectors, layer):
    return layer_norm(stream, vectors[6 * layer], vectors[6 * layer + 1])


def middle_piece(stream, mixed, vectors, layer):
    stream = stream + mixed + vectors[6 * layer + 4]
    return (stream, layer_norm(stream, vectors[6 * layer + 2], vectors[6 * layer + 3]))


def last_piece(stream, mixed, vectors, layer):
    return stream + mixed + vectors[6 * layer + 5]


def action_loss(stream, params, actions, lengths):
    rows = params["vectors"]
    base = 6 * LAYERS
    wins, steps = actions.shape
    final = layer_norm(stream, rows[base], rows[base + 1]).reshape(wins, steps, 3, D)[:, :, 1]
    logits = jnp.einsum("wsd,da->wsa", final, params["head"], precision=highest)
    peak = jnp.max(logits, -1, keepdims=True)
    total = jnp.log(jnp.sum(jnp.exp(logits - peak), -1)) + peak[..., 0]
    picked = jnp.sum(logits * jax.nn.one_hot(actions, ACT, dtype=jnp.float32), -1)
    valid = (jnp.arange(steps, dtype=jnp.int32)[None, :] < lengths[:, None]).astype(jnp.float32)
    return jnp.sum((total - picked) * valid)


def adam_update(weights, first, second, grads):
    first = beta_first * first + (1 - beta_first) * grads
    second = beta_second * second + (1 - beta_second) * grads * grads
    fix_one = 1 - beta_first**STEP
    fix_two = 1 - beta_second**STEP
    weights = weights - learn_rate * (
        first / fix_one / (jnp.sqrt(second / fix_two) + adam_epsilon) + weight_decay * weights
    )
    return (weights, first, second)


def per_device(
    frames,
    returns,
    actions,
    starts,
    lengths,
    shared_weights,
    shared_first,
    shared_second,
    split_weights,
    split_first,
    split_second,
):
    parts = lax.axis_size("mp")
    narrow = D // parts
    hidden_width = FF // parts

    def spread(normed):
        return (
            lax.all_gather(normed, "mp", axis=0, tiled=True),
            lax.all_gather(lengths, "mp", axis=0, tiled=True),
        )

    def collect(partial_sum):
        return lax.psum_scatter(partial_sum, "mp", scatter_dimension=0, tiled=True)

    def spread_back(grad):
        return lax.all_gather(grad, "mp", axis=0, tiled=True)

    def collect_back(grad):
        return lax.psum_scatter(grad, "mp", scatter_dimension=0, tiled=True)

    copies = 1
    layers, layers_back = jax.vjp(
        lambda flat: assemble(flat, copies, narrow, hidden_width), split_weights
    )
    params = unpack_shared(shared_weights)
    images = frames.astype(jnp.float32)

    def embed(table):
        return embed_tokens(table, images, returns, actions, starts)

    stream, embed_back = jax.vjp(embed, params)
    records = []
    for layer in range(LAYERS):
        weights = layers[layer]
        normed, back_one = jax.vjp(partial(first_piece, layer=layer), stream, params["vectors"])
        gathered, group_lengths = spread(normed)
        mixed, back_two = jax.vjp(
            partial(attention, lengths=group_lengths), gathered, weights["qkv"], weights["output"]
        )
        middle, back_three = jax.vjp(
            partial(middle_piece, layer=layer), stream, collect(mixed), params["vectors"]
        )
        gathered_two, unused = spread(middle[1])
        mixed_two, back_four = jax.vjp(
            feed_forward, gathered_two, weights["up"], weights["up_bias"], weights["down"]
        )
        stream, back_five = jax.vjp(
            partial(last_piece, layer=layer), middle[0], collect(mixed_two), params["vectors"]
        )
        records.append((back_one, back_two, back_three, back_four, back_five))

    def final_loss(stream_end, table):
        return action_loss(stream_end, table, actions, lengths)

    loss_local, loss_back = jax.vjp(final_loss, stream, params)
    count_local = jnp.sum(lengths).astype(jnp.float32)
    loss_sum, valid_count = lax.psum((loss_local, count_local), ("dp", "mp"))
    seed = 1.0 / valid_count
    grad_stream, grad_params = loss_back(seed.astype(jnp.float32))
    vector_grad = jnp.zeros_like(params["vectors"])
    grad_layers = [None] * LAYERS
    for layer in reversed(range(LAYERS)):
        back_one, back_two, back_three, back_four, back_five = records[layer]
        grad_middle, grad_mixed_two, grad_rows = back_five(grad_stream)
        grad_gathered_two, grad_up, grad_up_bias, grad_down = back_four(spread_back(grad_mixed_two))
        grad_stream, grad_mixed, grad_rows_two = back_three(
            (grad_middle, collect_back(grad_gathered_two))
        )
        grad_gathered, grad_qkv, grad_output = back_two(spread_back(grad_mixed))
        grad_stream_one, grad_rows_three = back_one(collect_back(grad_gathered))
        grad_stream = grad_stream + grad_stream_one
        vector_grad = vector_grad + grad_rows + grad_rows_two + grad_rows_three
        grad_layers[layer] = {
            "qkv": grad_qkv,
            "output": grad_output,
            "up": grad_up,
            "up_bias": grad_up_bias,
            "down": grad_down,
        }
    embed_grads = embed_back(grad_stream)[0]
    grads = jax.tree.map(jnp.add, grad_params, embed_grads)
    grads["vectors"] = grads["vectors"] + vector_grad
    shared_flat = pack_shared(grads, shared_weights.shape[0])
    layer_grad = layers_back(grad_layers)[0]
    split_sum = lax.psum(layer_grad, "dp")
    first_row = lax.axis_index("dp") == 0
    split_term = jnp.where(first_row, jnp.sum(split_sum * split_sum), 0.0)
    shared_sum = lax.psum(shared_flat, ("dp", "mp"))
    shared_term = jnp.where(
        first_row & (lax.axis_index("mp") == 0), jnp.sum(shared_sum * shared_sum), 0.0
    )
    squares = split_term + shared_term
    total_squares = lax.psum(squares, ("dp", "mp"))
    scale = jnp.ones((), jnp.float32)
    grad_norm = jnp.sqrt(total_squares) * scale
    factor = jnp.minimum(1.0, clip_limit / (grad_norm + 1e-06)) * scale
    split_new, split_m, split_v = adam_update(
        split_weights, split_first, split_second, split_sum * factor
    )
    shared_new, shared_m, shared_v = adam_update(
        shared_weights, shared_first, shared_second, shared_sum * factor
    )
    return (
        shared_new,
        shared_m,
        shared_v,
        shared_new.astype(jnp.bfloat16),
        split_new,
        split_m,
        split_v,
        split_new.astype(jnp.bfloat16),
        grad_norm,
        loss_sum,
        valid_count,
    )


def solution(mesh):
    return jax.shard_map(
        per_device,
        mesh=mesh,
        in_specs=(
            P(("dp", "mp"), None, None, None, None),
            P(("dp", "mp"), None),
            P(("dp", "mp"), None),
            P(("dp", "mp")),
            P(("dp", "mp")),
            P(),
            P(),
            P(),
            P("mp"),
            P("mp"),
            P("mp"),
        ),
        out_specs=(P(), P(), P(), P(), P("mp"), P("mp"), P("mp"), P("mp"), P(), P(), P()),
        check_vma=False,
    )
```

profile of v0, /device:TPU:0, one launch (start us, length us, event | category | flops | bytes accessed | tf_op | source)
XLA Modules:
  0.0 951.1 jit_solution(12094499645717614177)
XLA Ops:
  12.5 3.5 slice_bitcast_fusion
  16.2 21.7 %copy.102 = bf16[120,4,84,84]{0,1,3,2:T(4,128)(2,1)} copy(bf16[120,4,84,84]{3,1,2,0:T(4,128)(2,1)} %bitcast.283) | data formatting | bytes 13547520 | tf_op jit(solution)/shard_map/jvp()/reshape | solution.py:108
  38.5 6.7 reshape.607
  45.2 4.2 copy.75
  49.5 5.9 reshape.608
  55.4 7.4 copy.100
  62.8 19.9 %fusion.190 = f32[120,32,20,20]{0,1,3,2:T(8,128)S(1)} fusion(bf16[120,4,84,84]{0,1,3,2:T(4,128)(2,1)} %copy.102, f32[32,4,8,8]{0,1,3,2:T(4,128)S(1)} %copy.74), kind=kOutput, calls=%fused_computation.333 | convolution fusion | flops 4718592000 | bytes 12950528 | tf_op jit(solution)/shard_map/jvp()/conv_general_dilated | solution.py:95
  82.6 12.1 %fusion.72 = f32[120,64,9,9]{0,1,3,2:T(8,128)S(1)} fusion(f32[64,32,4,4]{0,1,3,2:T(8,128)S(1)} %copy.75, f32[120,32,20,20]{0,1,3,2:T(8,128)S(1)} %fusion.190, f32[32]{0:T(128)S(1)} %slice.178), kind=kOutput, calls=%fused_computation.120 | convolution fusion | flops 3835883520 | bytes 8763520 | tf_op jit(solution)/shard_map/jvp()/conv_general_dilated | solution.py:95
  94.8 9.9 %multiply_multiply_fusion.9 = (f32[120,64,7,7]{0,1,3,2:T(8,128)S(1)}, f32[120,64,7,7]{0,1,3,2:T(8,128)}) fusion(f32[64]{0:T(128)S(1)} %get-tuple-element.100, f32[64,64,3,3]{0,1,3,2:T(8,128)S(1)} %copy.100, f32[120,64,9,9]{0,1,3,2:T(8,128)S(1)} %fusion.72, f32[64]{0:T(128)S(1)} %get-tuple-element.99), kind=kOutput, calls=%fused_computation.53 | convolution fusion | flops 2610109440 | bytes 5646848 | tf_op jit(solution)/shard_map/jvp()/conv_general_dilated | solution.py:95
  105.8 4.7 fusion.28
  118.6 9.8 %all_gather.28 = f32[1440,128]{1,0:T(8,128)S(1)} all-gather(f32[360,128]{1,0:T(8,128)S(1)} %multiply_add_fusion.6), channel_id=1, replica_groups=mesh['dp'=8,'mp'=4] {'mp'}, dimensions={0}, use_global_device_ids=true | all-gather | bytes 921600 | tf_op jit(solution)/shard_map/all_gather | solution.py:218
  130.1 4.5 all-reduce.34
  151.3 20.4 %reduce-scatter.25.cloned.1.call-done = f32[360,128]{1,0:T(8,128)} async-done(((f32[1440,128]{1,0:T(8,128)}), f32[360,128]{1,0:T(8,128)}) %reduce-scatter.25.cloned.1.call-update) | async-done | bytes 184336
  174.0 8.3 all_gather.30
  188.1 22.7 %reduce-scatter.27.cloned.1.call-done = f32[360,128]{1,0:T(8,128)} async-done(((f32[1440,128]{1,0:T(8,128)}), f32[360,128]{1,0:T(8,128)}) %reduce-scatter.27.cloned.1.call-update) | async-done | bytes 184336
  213.5 8.4 all_gather.31
  227.0 3.8 fusion.185
  238.6 23.4 %reduce-scatter.29.cloned.1.call-done = f32[360,128]{1,0:T(8,128)} async-done(((f32[1440,128]{1,0:T(8,128)}), f32[360,128]{1,0:T(8,128)}) %reduce-scatter.29.cloned.1.call-update) | async-done | bytes 184336
  264.8 8.1 all_gather.32
  279.8 39.7 %psum.35 = f32[]{:T(128)} all-reduce(f32[]{:T(128)S(6)} %convert_element_type.23), channel_id=1, replica_groups=mesh['dp'=8,'mp'=4] {'dp','mp'}, use_global_device_ids=true, to_apply=%region_1.2 | all-reduce | flops 1 | bytes 8 | tf_op jit(solution)/shard_map/psum | solution.py:267
  344.1 9.3 all_gather.33
  359.0 20.5 %reduce-scatter.33.cloned.1.call-done = f32[360,128]{1,0:T(8,128)} async-done(((f32[1440,128]{1,0:T(8,128)}), f32[360,128]{1,0:T(8,128)}) %reduce-scatter.33.cloned.1.call-update) | async-done | bytes 184336
  385.8 8.6 all_gather.34
  399.3 4.1 convolution_bitcast_fusion.8
  416.0 3.8 fusion.195
  431.8 11.5 %reduce-scatter.35.cloned.1.call-done = f32[360,128]{1,0:T(8,128)} async-done(((f32[1440,128]{1,0:T(8,128)}), f32[360,128]{1,0:T(8,128)}) %reduce-scatter.35.cloned.1.call-update) | async-done | bytes 184336
  448.7 7.9 all_gather.35
  460.9 3.7 fusion.80
  464.6 3.2 fusion.198
  473.9 3.6 fusion.78
  479.6 4.8 reduce-scatter.37.cloned.1.call-done
  488.7 8.2 all_gather.36
  523.5 21.9 %reduce-scatter.39.cloned.1.call-done = f32[360,128]{1,0:T(8,128)} async-done(((f32[1440,128]{1,0:T(8,128)}), f32[360,128]{1,0:T(8,128)}) %reduce-scatter.39.cloned.1.call-update) | async-done | bytes 184336
  548.3 5.1 fusion.189
  553.5 12.0 %fusion.82 = f32[64,64,3,3]{0,1,3,2:T(8,128)S(1)} fusion(f32[120,64,7,7]{0,1,3,2:T(8,128)S(1)} %get-tuple-element.132, f32[120,64,9,9]{0,1,3,2:T(8,128)S(1)} %copy-done.140, f32[64]{0:T(128)S(1)} %copy-done.135), kind=kOutput, calls=%fused_computation.134 | convolution fusion | flops 2606722560 | bytes 4141312 | tf_op jit(solution)/shard_map/transpose(jvp())/conv_general_dilated | solution.py:95
  565.5 13.2 %fusion.188 = (f32[64]{0:T(128)}, f32[120,64,9,9]{0,1,3,2:T(8,128)S(1)}) fusion(f32[120,64,9,9]{0,1,3,2:T(8,128)S(1)} %copy-done.140, f32[64]{0:T(128)S(1)} %copy-done.135, f32[120,64,7,7]{0,1,3,2:T(8,128)S(1)} %get-tuple-element.132, f32[64,64,3,3]{0,1,3,2:T(8,128)S(1)} %copy-done.56), kind=kOutput, calls=%fused_computation.331 | convolution fusion | flops 2614187520 | bytes 6629888 | tf_op jit(solution)/shard_map/transpose(jvp())/conv_general_dilated | solution.py:95
  578.7 18.3 %fusion.71 = f32[64,32,4,4]{0,1,3,2:T(8,128)S(1)} fusion(f32[120,64,9,9]{0,1,3,2:T(8,128)S(1)} %get-tuple-element.130, f32[120,32,20,20]{0,1,3,2:T(8,128)S(1)} %bitcast.282, f32[32]{0:T(128)S(1)} %copy-done.138), kind=kOutput, calls=%fused_computation.119 | convolution fusion | flops 3835883520 | bytes 8763520 | tf_op jit(solution)/shard_map/transpose(jvp())/conv_general_dilated | solution.py:95
  597.0 43.2 %fusion.187 = (f32[32]{0:T(128)}, f32[120,32,20,20]{0,1,3,2:T(8,128)}) fusion(f32[120,32,20,20]{0,1,3,2:T(8,128)S(1)} %bitcast.282, f32[32]{0:T(128)S(1)} %copy-done.138, f32[120,64,9,9]{0,1,3,2:T(8,128)S(1)} %get-tuple-element.130, f32[64,32,4,4]{0,1,3,2:T(8,128)S(1)} %copy-done.58), kind=kOutput, calls=%fused_computation.330 | convolution fusion | flops 3854315520 | bytes 14907648 | tf_op jit(solution)/shard_map/transpose(jvp())/conv_general_dilated | solution.py:95
  640.5 8.2 copy.105
  648.7 7.4 reshape.625
  656.1 4.6 copy.104
  660.8 6.8 reshape.624
  667.5 32.1 %fusion.191 = f32[32,4,8,8]{0,1,3,2:T(4,128)S(1)} fusion(bf16[120,4,84,84]{0,1,3,2:T(4,128)(2,1)} %copy.102, f32[120,32,20,20]{0,1,3,2:T(8,128)} %get-tuple-element.128), kind=kOutput, calls=%fused_computation.334 | convolution fusion | flops 4718592000 | bytes 12950528 | tf_op jit(solution)/shard_map/transpose(jvp())/conv_general_dilated | solution.py:95
  705.2 39.9 %concatenate.3 = f32[1010688]{0:T(1024)} concatenate(f32[8192]{0:T(1024)S(1)} %reshape.623, f32[32]{0:T(128)} %get-tuple-element.127, f32[32768]{0:T(1024)} %reshape.624, f32[64]{0:T(128)} %get-tuple-element.129, f32[36864]{0:T(1024)S(1)} %reshape.625, f32[64]{0:T(128)} %get-tuple-element.131, f32[401408]{0:T(1024)S(1)} %convolution_bitcast_fusion, f32[2176]{0:T(1024)S(1)} %add_bitcast_fusion, ...), dimensions={0} | concatenate | bytes 8085504 | tf_op jit(solution)/shard_map/concatenate | solution.py:57
  747.6 138.8 %all-reduce.47.cloned.1.call-done = f32[1010688]{0:T(1024)} async-done(((f32[1010688]{0:T(1024)}), f32[1010688]{0:T(1024)}) %all-reduce.47.cloned.1.call-update) | async-done | bytes 4042768 | tf_op jit(solution)/shard_map/psum | solution.py:298
  886.4 3.8 multiply_reduce_fusion
  890.8 39.7 %all-reduce.43 = (f32[]{:T(128)}, f32[]{:T(128)}) all-reduce(f32[]{:T(128)S(6)} %add.552, f32[]{:T(128)} %get-tuple-element.114), channel_id=1, replica_groups=mesh['dp'=8,'mp'=4] {'dp','mp'}, use_global_device_ids=true, to_apply=%region_72.73 | all-reduce | flops 2 | bytes 16 | tf_op jit(solution)/shard_map/psum | solution.py:303
  932.6 10.1 %fusion.157 = (bf16[1010688]{0:T(1024)(128)(2,1)}, f32[1010688]{0:T(1024)}, f32[1010688]{0:T(1024)}, f32[1010688]{0:T(1024)}) fusion(f32[1010688]{0:T(1024)} %param.16, f32[1010688]{0:T(1024)} %all-reduce.47.cloned.1.call-done, f32[]{:T(128)S(6)} %min.3, f32[1010688]{0:T(1024)} %param.17, f32[1010688]{0:T(1024)} %param.18), kind=kLoop, calls=%fused_computation.303 | loop fusion | flops 17181696 | bytes 30320644 | tf_op jit(solution)/shard_map/convert_element_type | solution.py:317
  (495 shorter events, 189.4 us)
Async XLA Ops:
  7.2 164.6 %reduce-scatter.25.cloned.1.call-start = ((), (), s32[]{:S(2)}) async-start(), calls=%async_computation.10 | async-start | bytes 921600
  8.9 105.8 %copy-start.110 = (f32[128]{0:T(128)}, f32[128]{0:T(128)S(1)}, u32[]{:S(2)}) copy-start(f32[128]{0:T(128)S(1)} %get-tuple-element.97) | copy-start | bytes 1540
  9.0 105.8 %copy-start.112 = (f32[128]{0:T(128)}, f32[128]{0:T(128)S(1)}, u32[]{:S(2)}) copy-start(f32[128]{0:T(128)S(1)} %get-tuple-element.98) | copy-start | bytes 1540
  9.0 109.0 %copy-start.105 = (f32[128]{0:T(128)}, f32[128]{0:T(128)S(1)}, u32[]{:S(2)}) copy-start(f32[128]{0:T(128)S(1)} %get-tuple-element.95) | copy-start | bytes 1540
  9.7 73.0 %copy-start.137 = (f32[32]{0:T(128)}, f32[32]{0:T(128)S(1)}, u32[]{:S(2)}) copy-start(f32[32]{0:T(128)S(1)} %slice.178) | copy-start | bytes 388
  11.5 83.4 %copy-start.134 = (f32[64]{0:T(128)}, f32[64]{0:T(128)S(1)}, u32[]{:S(2)}) copy-start(f32[64]{0:T(128)S(1)} %get-tuple-element.99) | copy-start | bytes 772
  16.2 21.7 %slice-start = ((f32[1010688]{0:T(1024)}), f32[8192]{0:T(1024)S(1)}, s32[]{:S(2)}) async-start(f32[1010688]{0:T(1024)} %param.16), calls=%async_computation.18 | async-start | bytes 65536 | tf_op jit(solution)/shard_map/slice | solution.py:50
  49.5 33.2 %copy-start.57 = (f32[64,32,4,4]{0,1,3,2:T(8,128)}, f32[64,32,4,4]{0,1,3,2:T(8,128)S(1)}, u32[]{:S(2)}) copy-start(f32[64,32,4,4]{0,1,3,2:T(8,128)S(1)} %copy.75) | copy-start | bytes 393220
  62.8 32.1 %copy-start.55 = (f32[64,64,3,3]{0,1,3,2:T(8,128)}, f32[64,64,3,3]{0,1,3,2:T(8,128)S(1)}, u32[]{:S(2)}) copy-start(f32[64,64,3,3]{0,1,3,2:T(8,128)S(1)} %copy.100) | copy-start | bytes 442372
  117.3 27.5 %copy-start.71 = (f32[1,1,4096]{2,1,0:T(1,128)}, f32[1,1,4096]{2,1,0:T(1,128)S(1)}, u32[]{:S(2)}) copy-start(f32[1,1,4096]{2,1,0:T(1,128)S(1)} %get-tuple-element.110) | copy-start | bytes 49156
  117.7 18.9 %copy-start.87 = (f32[360]{0:T(512)}, f32[360]{0:T(512)S(1)}, u32[]{:S(2)}) copy-start(f32[360]{0:T(512)S(1)} %rsqrt.50) | copy-start | bytes 4324
  117.8 54.0 %copy-start.13 = (f32[360,128]{1,0:T(8,128)}, f32[360,128]{1,0:T(8,128)S(1)}, u32[]{:S(2)}) copy-start(f32[360,128]{1,0:T(8,128)S(1)} %add.499) | copy-start | bytes 552964
  142.2 31.0 %copy-start.107 = (f32[128]{0:T(128)S(1)}, f32[128]{0:T(128)}, u32[]{:S(2)}) copy-start(f32[128]{0:T(128)} %get-tuple-element.92) | copy-start | bytes 1540
  148.0 62.8 %reduce-scatter.27.cloned.1.call-start = ((), (), s32[]{:S(2)}) async-start(), calls=%async_computation.11 | async-start | bytes 921600
  173.1 14.1 %copy-start.97 = (f32[360]{0:T(512)}, f32[360]{0:T(512)S(1)}, u32[]{:S(2)}) copy-start(f32[360]{0:T(512)S(1)} %multiply_reduce_fusion.18) | copy-start | bytes 4324
  183.2 27.6 %copy-start.115 = (f32[128]{0:T(128)S(1)}, f32[128]{0:T(128)}, u32[]{:S(2)}) copy-start(f32[128]{0:T(128)} %get-tuple-element.90) | copy-start | bytes 1540
  187.2 74.8 %reduce-scatter.29.cloned.1.call-start = ((), (), s32[]{:S(2)}) async-start(), calls=%async_computation.12 | async-start | bytes 921600
  187.4 23.4 %copy-start.45 = (f32[128,96]{1,0:T(8,128)}, f32[128,96]{1,0:T(8,128)S(1)}, u32[]{:S(2)}) copy-start(f32[128,96]{1,0:T(8,128)S(1)} %squeeze.56) | copy-start | bytes 147460
  211.9 15.1 %copy-start.79 = (f32[360]{0:T(512)}, f32[360]{0:T(512)S(1)}, u32[]{:S(2)}) copy-start(f32[360]{0:T(512)S(1)} %broadcast_multiply_fusion.3) | copy-start | bytes 4324
  232.8 29.3 %copy-start.114 = (f32[128]{0:T(128)S(1)}, f32[128]{0:T(128)}, u32[]{:S(2)}) copy-start(f32[128]{0:T(128)} %get-tuple-element.87) | copy-start | bytes 1540
  238.6 84.5 %reduce-scatter.31.cloned.1.call-start = ((), (), s32[]{:S(2)}) async-start(), calls=%async_computation.13 | async-start | bytes 921600
  263.2 14.6 %copy-start.80 = (f32[360]{0:T(512)}, f32[360]{0:T(512)S(1)}, u32[]{:S(2)}) copy-start(f32[360]{0:T(512)S(1)} %broadcast_multiply_fusion.2) | copy-start | bytes 4324
  277.8 101.8 %reduce-scatter.33.cloned.1.call-start = ((), (), s32[]{:S(2)}) async-start(), calls=%async_computation.14 | async-start | bytes 921600
  338.9 14.5 %copy-start.41 = (f32[1440,128]{1,0:T(8,128)S(1)}, f32[1440,128]{1,0:T(8,128)}, u32[]{:S(2)}) copy-start(f32[1440,128]{1,0:T(8,128)} %copy-done.40) | copy-start | bytes 2211844
  338.9 14.5 %copy-start.77 = (f32[1,1,16384]{2,1,0:T(1,128)S(1)}, f32[1,1,16384]{2,1,0:T(1,128)}, u32[]{:S(2)}) copy-start(f32[1,1,16384]{2,1,0:T(1,128)} %get-tuple-element.103) | copy-start | bytes 196612
  357.7 85.6 %reduce-scatter.35.cloned.1.call-start = ((), (), s32[]{:S(2)}) async-start(), calls=%async_computation.15 | async-start | bytes 921600
  419.8 64.6 %reduce-scatter.37.cloned.1.call-start = ((), (), s32[]{:S(2)}) async-start(), calls=%async_computation.16 | async-start | bytes 921600
  460.9 84.6 %reduce-scatter.39.cloned.1.call-start = ((), (), s32[]{:S(2)}) async-start(), calls=%async_computation.17 | async-start | bytes 921600
  488.7 14.5 %copy-start.64 = (f32[16,2,90]{2,1,0:T(2,128)S(1)}, f32[16,2,90]{2,1,0:T(2,128)}, u32[]{:S(2)}) copy-start(f32[16,2,90]{2,1,0:T(2,128)} %copy-done.63) | copy-start | bytes 34564
  488.7 14.6 %copy-start.68 = (f32[16,2,90]{2,1,0:T(2,128)S(1)}, f32[16,2,90]{2,1,0:T(2,128)}, u32[]{:S(2)}) copy-start(f32[16,2,90]{2,1,0:T(2,128)} %copy-done.67) | copy-start | bytes 34564
  519.5 26.0 %copy-start.14 = (f32[360,128]{1,0:T(8,128)S(1)}, f32[360,128]{1,0:T(8,128)}, u32[]{:S(2)}) copy-start(f32[360,128]{1,0:T(8,128)} %copy-done.13) | copy-start | bytes 552964
  519.5 25.9 %copy-start.86 = (f32[360]{0:T(512)S(1)}, f32[360]{0:T(512)}, u32[]{:S(2)}) copy-start(f32[360]{0:T(512)} %copy-done.85) | copy-start | bytes 4324
  519.5 25.9 %copy-start.88 = (f32[360]{0:T(512)S(1)}, f32[360]{0:T(512)}, u32[]{:S(2)}) copy-start(f32[360]{0:T(512)} %copy-done.87) | copy-start | bytes 4324
  519.5 25.9 %copy-start.106 = (f32[128]{0:T(128)S(1)}, f32[128]{0:T(128)}, u32[]{:S(2)}) copy-start(f32[128]{0:T(128)} %copy-done.105) | copy-start | bytes 1540
  519.5 27.1 %copy-start.102 = (f32[360]{0:T(512)S(1)}, f32[360]{0:T(512)}, u32[]{:S(2)}) copy-start(f32[360]{0:T(512)} %copy-done.101) | copy-start | bytes 4324
  521.9 223.2 %all-reduce.49.cloned.1.call-start = ((), (), s32[]{:S(2)}) async-start(), calls=%async_computation.9 | async-start | bytes 794624 | tf_op jit(solution)/shard_map/psum | solution.py:295
  522.0 26.2 %copy-start.35 = (f32[120,128]{1,0:T(8,128)S(1)}, f32[120,128]{1,0:T(8,128)}, u32[]{:S(2)}) copy-start(f32[120,128]{1,0:T(8,128)} %copy-done.34) | copy-start | bytes 184324
  523.5 362.9 %all-reduce.47.cloned.1.call-start = ((), (), s32[]{:S(2)}) async-start(), calls=%async_computation.8 | async-start | bytes 8085504 | tf_op jit(solution)/shard_map/psum | solution.py:298
  548.3 30.3 %slice-start.1 = ((s8[6553600]{0:T(1024)(128)(4,1)}), s8[4194304]{0:T(1024)(128)(4,1)S(1)}, s32[]{:S(2)}) async-start(s8[6553600]{0:T(1024)(128)(4,1)} %bitcast.281), calls=%async_computation.19 | async-start | bytes 8388608
  553.5 25.2 %slice-start.2 = ((s8[6553600]{0:T(1024)(128)(4,1)}), s8[2359296]{0:T(1024)(128)(4,1)S(1)}, s32[]{:S(2)}) async-start(s8[6553600]{0:T(1024)(128)(4,1)} %bitcast.281), calls=%async_computation.20 | async-start | bytes 4718592
  578.6 18.3 %copy-start.58 = (f32[64,32,4,4]{0,1,3,2:T(8,128)S(1)}, f32[64,32,4,4]{0,1,3,2:T(8,128)}, u32[]{:S(2)}) copy-start(f32[64,32,4,4]{0,1,3,2:T(8,128)} %copy-done.57) | copy-start | bytes 393220
  597.0 43.4 %copy-start.109 = (f32[4,30]{1,0:T(4,128)S(1)}, f32[4,30]{1,0:T(4,128)}, u32[]{:S(2)}) copy-start(f32[4,30]{1,0:T(4,128)} %param.12) | copy-start | bytes 1444
  597.0 43.4 %copy-start.111 = (f32[128]{0:T(128)S(1)}, f32[128]{0:T(128)}, u32[]{:S(2)}) copy-start(f32[128]{0:T(128)} %copy-done.110) | copy-start | bytes 1540
  597.0 43.4 %copy-start.113 = (f32[128]{0:T(128)S(1)}, f32[128]{0:T(128)}, u32[]{:S(2)}) copy-start(f32[128]{0:T(128)} %copy-done.112) | copy-start | bytes 1540
  746.8 184.4 %copy-start.30 = (f32[98560]{0:T(1024)S(1)}, f32[98560]{0:T(1024)}, u32[]{:S(2)}) copy-start(f32[98560]{0:T(1024)} %param.19) | copy-start | bytes 1182724
  746.8 184.4 %copy-start.31 = (f32[98560]{0:T(1024)S(1)}, f32[98560]{0:T(1024)}, u32[]{:S(2)}) copy-start(f32[98560]{0:T(1024)} %all-reduce.49.cloned.1.call-done) | copy-start | bytes 1182724
  746.8 184.5 %copy-start.53 = (f32[98560]{0:T(1024)S(1)}, f32[98560]{0:T(1024)}, u32[]{:S(2)}) copy-start(f32[98560]{0:T(1024)} %param.20) | copy-start | bytes 1182724
  746.8 184.5 %copy-start.54 = (f32[98560]{0:T(1024)S(1)}, f32[98560]{0:T(1024)}, u32[]{:S(2)}) copy-start(f32[98560]{0:T(1024)} %param.21) | copy-start | bytes 1182724
  (106 other events, 488.9 us)
Sparse Core Ops, SparseCore 0:
  148.1 23.6 reduce-scatter.24
  187.4 23.3 reduce-scatter.26
  238.7 23.3 reduce-scatter.28
  277.9 23.3 reduce-scatter.30
  357.8 21.7 reduce-scatter.32
  419.9 23.3 reduce-scatter.34
  461.0 23.3 reduce-scatter.36
  522.0 23.3 reduce-scatter.38
  549.4 71.6 all-reduce.48
  745.2 141.1 all-reduce.46
where the time goes:
time: 965 us; the launch traced here: 951 us
  matrix products  265 us (27%)
  waiting for transfers between devices  264 us (27%)
  local copies, waits for them, and re-layouts  184 us (19%)
  blocking collectives  153 us (16%)
  other arithmetic  63.4 us (7%)
  between operations  22.1 us (2%)
    conv_general_dilated x8, matrix products, conv_layer(): lax.conv_general_dilated(images, kernel, (stride, stride), 'VALID', dimen...  161 us
    psum x1, waiting for transfers between devices, per_device(): shared_sum = lax.psum(shared_flat, ('dp', 'mp'))  139 us
    unnamed x18, waiting for transfers between devices  125 us
    concatenate x1, local copies, waits for them, and re-layouts, pack_shared(): jnp.concatenate([flat, jnp.zeros((total - flat.shape[0],), jnp.float32)])  39.9 us
    psum x1, blocking collectives, per_device(): loss_sum, valid_count = lax.psum((loss_local, count_local), ('dp', 'mp'))  39.7 us
    psum x1, blocking collectives, per_device(): total_squares = lax.psum(squares, ('dp', 'mp'))  39.7 us
    all_gather x4, blocking collectives, spread(): lax.all_gather(normed, 'mp', axis=0, tiled=True)  34.6 us
    all_gather x4, blocking collectives, spread_back(): return lax.all_gather(grad, 'mp', axis=0, tiled=True)  34.1 us
  transfers between devices with their start and end apart: 10, of which 8 were waited for; matrix products, arithmetic and copies ran while one was open for 25% of the time, Pallas kernels for 0%

commit v1 on v0

--- a/solution.py
+++ b/solution.py
@@ -17,7 +17,7 @@
 HD = 16
 
 
-highest = lax.Precision.HIGHEST
+high = lax.Precision.HIGH
 clip_limit = 0.1
 learn_rate = 0.05
 beta_first = 0.9
@@ -98,7 +98,7 @@
         (stride, stride),
         "VALID",
         dimension_numbers=("NCHW", "OIHW", "NCHW"),
-        precision=highest,
+        precision=high,
     )
     return jax.nn.gelu(result + bias[None, :, None, None])
 
@@ -112,13 +112,13 @@
     rows = params["vectors"]
     base = 6 * LAYERS
     states = jnp.tanh(
-        jnp.dot(hidden.reshape(wins * steps, -1), params["encoder"], precision=highest)
+        jnp.dot(hidden.reshape(wins * steps, -1), params["encoder"], precision=high)
         + rows[base + 4]
     )
     states = states.reshape(wins, steps, D)
     rewards = jnp.tanh(returns[:, :, None] * rows[base + 2] + rows[base + 3])
     picks = jax.nn.one_hot(actions, ACT, dtype=jnp.float32)
-    moves = jnp.tanh(jnp.einsum("wsa,ad->wsd", picks, params["action_table"], precision=highest))
+    moves = jnp.tanh(jnp.einsum("wsa,ad->wsd", picks, params["action_table"], precision=high))
     places = starts[:, None] + jnp.arange(steps, dtype=jnp.int32)[None, :]
     times = jnp.take(params["time_table"], places, axis=0)
     tokens = jnp.stack([rewards, states, moves], axis=2) + times[:, :, None, :]
@@ -135,11 +135,11 @@
     wins = lengths.shape[0]
     tokens = normed.shape[0] // wins
     heads = qkv.shape[-1] // HD
-    mixed = jnp.dot(normed, qkv.reshape(D, -1), precision=highest).reshape(
+    mixed = jnp.dot(normed, qkv.reshape(D, -1), precision=high).reshape(
         wins, tokens, 3, heads, HD
     )
     query, keys, values = (mixed[:, :, 0], mixed[:, :, 1], mixed[:, :, 2])
-    scores = jnp.einsum("wqhe,wkhe->whqk", query, keys, precision=highest) * HD ** (-0.5)
+    scores = jnp.einsum("wqhe,wkhe->whqk", query, keys, precision=high) * HD ** (-0.5)
     place = jnp.arange(tokens, dtype=jnp.int32)
     allowed = (place[None, :, None] >= place[None, None, :]) & (
         place[None, None, :] < 3 * lengths[:, None, None]
@@ -148,15 +148,15 @@
     peak = jnp.max(scores, -1, keepdims=True)
     weights = jnp.exp(scores - peak)
     weights = weights / jnp.sum(weights, -1, keepdims=True)
-    context = jnp.einsum("whqk,wkhe->wqhe", weights, values, precision=highest).reshape(
+    context = jnp.einsum("whqk,wkhe->wqhe", weights, values, precision=high).reshape(
         wins * tokens, heads * HD
     )
-    return jnp.dot(context, output, precision=highest)
+    return jnp.dot(context, output, precision=high)
 
 
 def feed_forward(normed, up, up_bias, down):
-    inner = jax.nn.gelu(jnp.dot(normed, up, precision=highest) + up_bias)
-    return jnp.dot(inner, down, precision=highest)
+    inner = jax.nn.gelu(jnp.dot(normed, up, precision=high) + up_bias)
+    return jnp.dot(inner, down, precision=high)
 
 
 def first_piece(stream, vectors, layer):
@@ -177,7 +177,7 @@
     base = 6 * LAYERS
     wins, steps = actions.shape
     final = layer_norm(stream, rows[base], rows[base + 1]).reshape(wins, steps, 3, D)[:, :, 1]
-    logits = jnp.einsum("wsd,da->wsa", final, params["head"], precision=highest)
+    logits = jnp.einsum("wsd,da->wsa", final, params["head"], precision=high)
     peak = jnp.max(logits, -1, keepdims=True)
     total = jnp.log(jnp.sum(jnp.exp(logits - peak), -1)) + peak[..., 0]
     picked = jnp.sum(logits * jax.nn.one_hot(actions, ACT, dtype=jnp.float32), -1)
@@ -212,103 +212,46 @@
     parts = lax.axis_size("mp")
     narrow = D // parts
     hidden_width = FF // parts
-
-    def spread(normed):
-        return (
-            lax.all_gather(normed, "mp", axis=0, tiled=True),
-            lax.all_gather(lengths, "mp", axis=0, tiled=True),
-        )
-
-    def collect(partial_sum):
-        return lax.psum_scatter(partial_sum, "mp", scatter_dimension=0, tiled=True)
-
-    def spread_back(grad):
-        return lax.all_gather(grad, "mp", axis=0, tiled=True)
-
-    def collect_back(grad):
-        return lax.psum_scatter(grad, "mp", scatter_dimension=0, tiled=True)
-
-    copies = 1
-    layers, layers_back = jax.vjp(
-        lambda flat: assemble(flat, copies, narrow, hidden_width), split_weights
-    )
+    split_all = lax.all_gather(split_weights, "mp", axis=0, tiled=True)
     params = unpack_shared(shared_weights)
     images = frames.astype(jnp.float32)
 
-    def embed(table):
-        return embed_tokens(table, images, returns, actions, starts)
-
-    stream, embed_back = jax.vjp(embed, params)
-    records = []
-    for layer in range(LAYERS):
-        weights = layers[layer]
-        normed, back_one = jax.vjp(partial(first_piece, layer=layer), stream, params["vectors"])
-        gathered, group_lengths = spread(normed)
-        mixed, back_two = jax.vjp(
-            partial(attention, lengths=group_lengths), gathered, weights["qkv"], weights["output"]
-        )
-        middle, back_three = jax.vjp(
-            partial(middle_piece, layer=layer), stream, collect(mixed), params["vectors"]
-        )
-        gathered_two, unused = spread(middle[1])
-        mixed_two, back_four = jax.vjp(
-            feed_forward, gathered_two, weights["up"], weights["up_bias"], weights["down"]
-        )
-        stream, back_five = jax.vjp(
-            partial(last_piece, layer=layer), middle[0], collect(mixed_two), params["vectors"]
-        )
-        records.append((back_one, back_two, back_three, back_four, back_five))
-
-    def final_loss(stream_end, table):
-        return action_loss(stream_end, table, actions, lengths)
-
-    loss_local, loss_back = jax.vjp(final_loss, stream, params)
+    def local_loss(table, flat):
+        layers = assemble(flat, parts, narrow, hidden_width)
+        stream = embed_tokens(table, images, returns, actions, starts)
+        for layer in range(LAYERS):
+            weights = layers[layer]
+            normed = first_piece(stream, table["vectors"], layer)
+            mixed = attention(normed, weights["qkv"], weights["output"], lengths)
+            stream, normed = middle_piece(stream, mixed, table["vectors"], layer)
+            mixed = feed_forward(normed, weights["up"], weights["up_bias"], weights["down"])
+            stream = last_piece(stream, mixed, table["vectors"], layer)
+        return action_loss(stream, table, actions, lengths)
+
+    loss_local, (grads, split_grad) = jax.value_and_grad(local_loss, argnums=(0, 1))(
+        params, split_all
+    )
     count_local = jnp.sum(lengths).astype(jnp.float32)
-    loss_sum, valid_count = lax.psum((loss_local, count_local), ("dp", "mp"))
+    pieces = [grads[name].reshape(-1) for name, shape in shared_layout()]
+    raw = sum(piece.shape[0] for piece in pieces)
+    total = shared_weights.shape[0]
+    tail = jnp.zeros((total - raw,), jnp.float32)
+    scalars = jnp.stack([loss_local, count_local])
+    flat = jnp.concatenate(pieces + [tail, split_grad, scalars])
+    summed = lax.psum(flat, ("dp", "mp"))
+    loss_sum = summed[-2]
+    valid_count = summed[-1]
     seed = 1.0 / valid_count
-    grad_stream, grad_params = loss_back(seed.astype(jnp.float32))
-    vector_grad = jnp.zeros_like(params["vectors"])
-    grad_layers = [None] * LAYERS
-    for layer in reversed(range(LAYERS)):
-        back_one, back_two, back_three, back_four, back_five = records[layer]
-        grad_middle, grad_mixed_two, grad_rows = back_five(grad_stream)
-        grad_gathered_two, grad_up, grad_up_bias, grad_down = back_four(spread_back(grad_mixed_two))
-        grad_stream, grad_mixed, grad_rows_two = back_three(
-            (grad_middle, collect_back(grad_gathered_two))
-        )
-        grad_gathered, grad_qkv, grad_output = back_two(spread_back(grad_mixed))
-        grad_stream_one, grad_rows_three = back_one(collect_back(grad_gathered))
-        grad_stream = grad_stream + grad_stream_one
-        vector_grad = vector_grad + grad_rows + grad_rows_two + grad_rows_three
-        grad_layers[layer] = {
-            "qkv": grad_qkv,
-            "output": grad_output,
-            "up": grad_up,
-            "up_bias": grad_up_bias,
-            "down": grad_down,
-        }
-    embed_grads = embed_back(grad_stream)[0]
-    grads = jax.tree.map(jnp.add, grad_params, embed_grads)
-    grads["vectors"] = grads["vectors"] + vector_grad
-    shared_flat = pack_shared(grads, shared_weights.shape[0])
-    layer_grad = layers_back(grad_layers)[0]
-    split_sum = lax.psum(layer_grad, "dp")
-    first_row = lax.axis_index("dp") == 0
-    split_term = jnp.where(first_row, jnp.sum(split_sum * split_sum), 0.0)
-    shared_sum = lax.psum(shared_flat, ("dp", "mp"))
-    shared_term = jnp.where(
-        first_row & (lax.axis_index("mp") == 0), jnp.sum(shared_sum * shared_sum), 0.0
-    )
-    squares = split_term + shared_term
-    total_squares = lax.psum(squares, ("dp", "mp"))
-    scale = jnp.ones((), jnp.float32)
-    grad_norm = jnp.sqrt(total_squares) * scale
-    factor = jnp.minimum(1.0, clip_limit / (grad_norm + 1e-06)) * scale
+    summed = summed[:-2] * seed
+    grad_norm = jnp.sqrt(jnp.sum(summed * summed))
+    factor = jnp.minimum(1.0, clip_limit / (grad_norm + 1e-06))
+    width = split_weights.shape[0]
+    split_sum = lax.dynamic_slice(summed, (total + lax.axis_index("mp") * width,), (width,))
     split_new, split_m, split_v = adam_update(
         split_weights, split_first, split_second, split_sum * factor
     )
     shared_new, shared_m, shared_v = adam_update(
-        shared_weights, shared_first, shared_second, shared_sum * factor
+        shared_weights, shared_first, shared_second, summed[:total] * factor
     )
     return (
         shared_new,

time: 965 us -> 598 us (0.62)
  blocking collectives: 153 us -> 0 us
  waiting for transfers between devices: 264 us -> 154 us
  matrix products: 265 us -> 162 us
  local copies, waits for them, and re-layouts: 184 us -> 201 us
  other arithmetic: 63.4 us -> 50.1 us
    unnamed x18 -> x2, waiting for transfers between devices: 125 us -> 0.03 us
    psum x2 -> x0, blocking collectives: 79.4 us -> none  [the longest x1 39.7 us: per_device(): loss_sum, valid_count = lax.psum((loss_local, count_local), ('dp', 'mp'))]
    all_gather x8 -> x0, blocking collectives: 68.7 us -> none  [the longest x4 34.6 us: spread(): lax.all_gather(normed, 'mp', axis=0, tiled=True)]
    conv_general_dilated x8, matrix products: 161 us -> 97.8 us  [conv_layer(): lax.conv_general_dilated(images, kernel, (stride, stride), 'VALID', dimen...]
    dot_general x44, matrix products: 104 us -> 63.9 us  [the longest x6 11.2 us: feed_forward(): return jnp.dot(inner, down, precision=high)]
    psum x2 -> x1, waiting for transfers between devices: 139 us -> 153 us  [per_device(): summed = lax.psum(flat, ('dp', 'mp'))]
    concatenate x1, local copies, waits for them, and re-layouts: 39.9 us -> 51 us  [per_device(): flat = jnp.concatenate(pieces + [tail, split_grad, scalars])]
    reshape x8 -> x10, local copies, waits for them, and re-layouts: 23.2 us -> 20.4 us  [the longest x4 13.9 us: per_device(): pieces = [grads[name].reshape(-1) for name, shape in shared_layout()]]
  transfers between devices with their start and end apart: 10 -> 2, of which waited for: 8 -> 1; matrix products, arithmetic and copies ran while one was open for 25% -> 18% of each run, Pallas kernels for 0% -> 0%
where the time goes in v1:
time: 598 us; the launch traced here: 587 us
  local copies, waits for them, and re-layouts  201 us (34%)
  matrix products  162 us (27%)
  waiting for transfers between devices  154 us (26%)
  other arithmetic  50.1 us (8%)
  between operations  20 us (3%)
    psum x1, waiting for transfers between devices, per_device(): summed = lax.psum(flat, ('dp', 'mp'))  153 us
    conv_general_dilated x8, matrix products, conv_layer(): lax.conv_general_dilated(images, kernel, (stride, stride), 'VALID', dimen...  97.8 us
    concatenate x1, local copies, waits for them, and re-layouts, per_device(): flat = jnp.concatenate(pieces + [tail, split_grad, scalars])  51 us
    reshape x8, local copies, waits for them, and re-layouts, unpack_shared(): params[name] = flat[offset:offset + count].reshape(shape)  29.3 us
    reshape x1, local copies, waits for them, and re-layouts, embed_tokens(): images = frames.reshape(wins * steps, 4, 84, 84)  21.7 us
    reshape x4, local copies, waits for them, and re-layouts, per_device(): pieces = [grads[name].reshape(-1) for name, shape in shared_layout()]  13.9 us
    conv_general_dilated x3, local copies, waits for them, and re-layouts, conv_layer(): lax.conv_general_dilated(images, kernel, (stride, stride), 'VALID', dimen...  13.4 us
  transfers between devices with their start and end apart: 2, of which 1 were waited for; matrix products, arithmetic and copies ran while one was open for 18% of the time, Pallas kernels for 0%

profile of v1, /device:TPU:0, one launch (start us, length us, event | category | flops | bytes accessed | tf_op | source)
XLA Modules:
  0.0 586.6 jit_solution(11701190889094155824)
XLA Ops:
  7.2 2.0 reshape.852
  14.6 3.7 slice_bitcast_fusion
  19.1 21.7 %copy.155 = bf16[120,4,84,84]{0,1,3,2:T(4,128)(2,1)} copy(bf16[120,4,84,84]{3,1,2,0:T(4,128)(2,1)} %bitcast.293) | data formatting | bytes 13547520 | tf_op jit(solution)/shard_map/jvp()/reshape | solution.py:108
  41.5 6.7 %reshape.778 = f32[64,32,4,4]{3,2,1,0:T(4,128)} reshape(f32[32768]{0:T(1024)S(1)} %slice.191) | data formatting | bytes 262144 | tf_op jit(solution)/shard_map/reshape | solution.py:50
  48.2 4.2 copy.124
  52.5 5.9 %reshape.779 = f32[64,64,3,3]{3,2,1,0:T(4,128)} reshape(f32[36864]{0:T(1024)S(1)} %slice.193) | data formatting | bytes 294912 | tf_op jit(solution)/shard_map/reshape | solution.py:50
  58.4 7.4 %copy.153 = f32[64,64,3,3]{0,1,3,2:T(8,128)S(1)} copy(f32[64,64,3,3]{3,2,1,0:T(4,128)} %reshape.779) | data formatting | bytes 294912 | tf_op jit(solution)/shard_map/reshape | solution.py:50
  65.7 14.7 %fusion.221 = f32[120,32,20,20]{0,1,3,2:T(8,128)S(1)} fusion(bf16[120,4,84,84]{0,1,3,2:T(4,128)(2,1)} %copy.155, f32[32,4,8,8]{0,1,3,2:T(4,128)S(1)} %copy.123), kind=kOutput, calls=%fused_computation.368 | convolution fusion | flops 2359296000 | bytes 12950528 | tf_op jit(solution)/shard_map/jvp()/conv_general_dilated | solution.py:95
  80.4 6.9 %fusion.70 = f32[120,64,9,9]{0,1,3,2:T(8,128)S(1)} fusion(f32[64,32,4,4]{0,1,3,2:T(8,128)S(1)} %copy.124, f32[120,32,20,20]{0,1,3,2:T(8,128)S(1)} %fusion.221, f32[32]{0:T(128)S(1)} %slice.190), kind=kOutput, calls=%fused_computation.127 | convolution fusion | flops 1924853760 | bytes 8763520 | tf_op jit(solution)/shard_map/jvp()/conv_general_dilated | solution.py:95
  87.4 6.0 %multiply_multiply_fusion.9 = (f32[120,64,7,7]{0,1,3,2:T(8,128)S(1)}, f32[120,64,7,7]{0,1,3,2:T(8,128)}) fusion(f32[64]{0:T(128)S(1)} %get-tuple-element.88, f32[64,64,3,3]{0,1,3,2:T(8,128)S(1)} %copy.153, f32[120,64,9,9]{0,1,3,2:T(8,128)S(1)} %fusion.70, f32[64]{0:T(128)S(1)} %get-tuple-element.87), kind=kOutput, calls=%fused_computation.54 | convolution fusion | flops 1309547520 | bytes 5646848 | tf_op jit(solution)/shard_map/jvp()/conv_general_dilated | solution.py:95
  94.5 3.5 fusion.32
  98.7 2.2 gather_fusion
  105.2 1.9 slice.195
  115.3 6.7 %reduce.3 = f32[4,98560]{1,0:T(4,128)} reduce(f32[4,1,98560]{2,1,0:T(1,128)} %all-gather.3.cloned.1.call-done, f32[]{:T(128)} %constant.212), dimensions={1}, to_apply=%all-gather.reduce_sub_computation | reduce | bytes 3153924 | tf_op jit(solution)/shard_map/all_gather | solution.py:215
  122.0 2.7 reshape.785
  127.2 2.0 fusion.204
  136.5 1.8 reshape.787
  143.2 1.8 fusion.211
  146.9 2.6 squeeze.62
  149.5 2.1 copy.134
  153.2 2.3 fusion.212
  166.4 2.1 fusion.214
  182.3 1.9 multiply_reduce_fusion.8
  186.2 2.7 fusion.77
  197.6 2.9 convolution_bitcast_fusion.8
  200.5 1.9 convert_reduce_fusion.1
  207.2 2.3 reshape.795
  209.7 2.6 multiply_reduce_fusion.6
  225.0 1.9 convert_reduce_fusion
  233.0 2.5 multiply_reduce_fusion.4
  236.8 1.9 convolution_bitcast_fusion
  238.7 2.5 fusion.218
  241.2 6.8 %fusion.78 = f32[64,64,3,3]{0,1,3,2:T(8,128)} fusion(f32[120,64,7,7]{0,1,3,2:T(8,128)S(1)} %get-tuple-element.137, f32[120,64,9,9]{0,1,3,2:T(8,128)S(1)} %copy-done.149, f32[64]{0:T(128)S(1)} %copy-done.145), kind=kOutput, calls=%fused_computation.137 | convolution fusion | flops 1306160640 | bytes 4141312 | tf_op jit(solution)/shard_map/transpose(jvp())/conv_general_dilated | solution.py:95
  248.0 8.0 %fusion.217 = (f32[64]{0:T(128)}, f32[120,64,9,9]{0,1,3,2:T(8,128)S(1)}) fusion(f32[120,64,9,9]{0,1,3,2:T(8,128)S(1)} %copy-done.149, f32[64]{0:T(128)S(1)} %copy-done.145, f32[120,64,7,7]{0,1,3,2:T(8,128)S(1)} %get-tuple-element.137, f32[64,64,3,3]{0,1,3,2:T(8,128)S(1)} %copy-done.50), kind=kOutput, calls=%fused_computation.364 | convolution fusion | flops 1313625600 | bytes 6629888 | tf_op jit(solution)/shard_map/transpose(jvp())/conv_general_dilated | solution.py:95
  256.1 10.0 %fusion.69 = f32[64,32,4,4]{0,1,3,2:T(8,128)} fusion(f32[120,64,9,9]{0,1,3,2:T(8,128)S(1)} %get-tuple-element.135, f32[120,32,20,20]{0,1,3,2:T(8,128)S(1)} %bitcast.292, f32[32]{0:T(128)S(1)} %copy-done.147), kind=kOutput, calls=%fused_computation.126 | convolution fusion | flops 1924853760 | bytes 8763520 | tf_op jit(solution)/shard_map/transpose(jvp())/conv_general_dilated | solution.py:95
  266.1 23.0 %fusion.216 = (f32[32]{0:T(128)}, f32[120,32,20,20]{0,1,3,2:T(8,128)}) fusion(f32[120,32,20,20]{0,1,3,2:T(8,128)S(1)} %bitcast.292, f32[32]{0:T(128)S(1)} %copy-done.147, f32[120,64,9,9]{0,1,3,2:T(8,128)S(1)} %get-tuple-element.135, f32[64,32,4,4]{0,1,3,2:T(8,128)S(1)} %copy-done.53), kind=kOutput, calls=%fused_computation.363 | convolution fusion | flops 1943285760 | bytes 14907648 | tf_op jit(solution)/shard_map/transpose(jvp())/conv_general_dilated | solution.py:95
  294.7 2.6 pad_add_fusion
  298.2 2.4 reshape.833
  300.9 8.2 %copy.158 = f32[64,64,3,3]{3,2,1,0:T(4,128)} copy(f32[64,64,3,3]{0,1,3,2:T(8,128)S(1)} %copy-done.51) | data formatting | bytes 294912 | tf_op jit(solution)/shard_map/transpose(jvp())/conv_general_dilated | solution.py:95
  309.1 7.4 %reshape.800 = f32[36864]{0:T(1024)S(1)} reshape(f32[64,64,3,3]{3,2,1,0:T(4,128)} %copy.158) | data formatting | bytes 294912 | tf_op jit(solution)/shard_map/reshape | solution.py:235
  316.6 4.7 copy.157
  321.2 6.1 %reshape.799 = f32[32768]{0:T(1024)S(1)} reshape(f32[64,32,4,4]{3,2,1,0:T(4,128)} %copy.157) | data formatting | bytes 262144 | tf_op jit(solution)/shard_map/reshape | solution.py:235
  327.4 22.3 %fusion.222 = f32[32,4,8,8]{0,1,3,2:T(4,128)S(1)} fusion(bf16[120,4,84,84]{0,1,3,2:T(4,128)(2,1)} %copy.155, f32[120,32,20,20]{0,1,3,2:T(8,128)} %get-tuple-element.133), kind=kOutput, calls=%fused_computation.369 | convolution fusion | flops 2359296000 | bytes 12950528 | tf_op jit(solution)/shard_map/transpose(jvp())/conv_general_dilated | solution.py:95
  352.7 51.0 %concatenate.3 = f32[1404930]{0:T(1024)} concatenate(f32[8192]{0:T(1024)S(1)} %reshape.798, f32[32]{0:T(128)S(1)} %copy-done.142, f32[32768]{0:T(1024)S(1)} %reshape.799, f32[64]{0:T(128)S(1)} %copy-done.141, f32[36864]{0:T(1024)S(1)} %reshape.800, f32[64]{0:T(128)S(1)} %copy-done.140, f32[401408]{0:T(1024)} %convolution_bitcast_fusion, f32[2176]{0:T(1024)S(1)} %add_bitcast_fusion, ...), dimensions={0} | concatenate | bytes 11239440 | tf_op jit(solution)/shard_map/concatenate | solution.py:240
  403.7 153.5 %all-reduce.36.cloned.1.call-done = f32[1404930]{0:T(1024)} async-done(((f32[1404930]{0:T(1024)}), f32[1404930]{0:T(1024)}) %all-reduce.36.cloned.1.call-update) | async-done | bytes 5619736 | tf_op jit(solution)/shard_map/psum | solution.py:241
  559.2 5.5 multiply_reduce_fusion
  565.5 10.2 %fusion.188 = (bf16[1010688]{0:T(1024)(128)(2,1)}, f32[1010688]{0:T(1024)}, f32[1010688]{0:T(1024)}, f32[1010688]{0:T(1024)}) fusion(f32[1010688]{0:T(1024)} %param.16, f32[]{:T(128)S(6)} %min.3, f32[1404928]{0:T(1024)} %get-tuple-element.41, f32[1010688]{0:T(1024)} %param.17, f32[1010688]{0:T(1024)} %param.18), kind=kLoop, calls=%fused_computation.336 | loop fusion | flops 17181696 | bytes 30320644 | tf_op jit(solution)/shard_map/convert_element_type | solution.py:260
  575.7 2.5 fusion.186
  (480 shorter events, 108.2 us)
Async XLA Ops:
  7.2 108.2 %all-gather.3.cloned.1.call-start = ((), (), s32[]{:S(2)}) async-start(), calls=%async_computation.1 | async-start | bytes 1971200 | tf_op jit(solution)/shard_map/all_gather | solution.py:215
  9.3 548.0 %all-reduce.36.cloned.1.call-start = ((), (), s32[]{:S(2)}) async-start(), calls=%async_computation | async-start | bytes 11247616 | tf_op jit(solution)/shard_map/psum | solution.py:241
  11.0 87.1 %copy-start.111 = (f32[128]{0:T(128)}, f32[128]{0:T(128)S(1)}, u32[]{:S(2)}) copy-start(f32[128]{0:T(128)S(1)} %get-tuple-element.85) | copy-start | bytes 1540
  11.1 87.1 %copy-start.113 = (f32[128]{0:T(128)}, f32[128]{0:T(128)S(1)}, u32[]{:S(2)}) copy-start(f32[128]{0:T(128)S(1)} %get-tuple-element.86) | copy-start | bytes 1540
  11.1 92.2 %copy-start.105 = (f32[128]{0:T(128)}, f32[128]{0:T(128)S(1)}, u32[]{:S(2)}) copy-start(f32[128]{0:T(128)S(1)} %get-tuple-element.83) | copy-start | bytes 1540
  11.1 130.7 %copy-start.102 = (f32[128]{0:T(128)}, f32[128]{0:T(128)S(1)}, u32[]{:S(2)}) copy-start(f32[128]{0:T(128)S(1)} %get-tuple-element.80) | copy-start | bytes 1540
  11.8 68.6 %copy-start.146 = (f32[32]{0:T(128)}, f32[32]{0:T(128)S(1)}, u32[]{:S(2)}) copy-start(f32[32]{0:T(128)S(1)} %slice.190) | copy-start | bytes 388
  13.6 73.8 %copy-start.144 = (f32[64]{0:T(128)}, f32[64]{0:T(128)S(1)}, u32[]{:S(2)}) copy-start(f32[64]{0:T(128)S(1)} %get-tuple-element.87) | copy-start | bytes 772
  14.6 3.7 copy-start.143
  14.6 3.8 copy-start
  19.1 21.7 %slice-start = ((f32[1010688]{0:T(1024)}), f32[8192]{0:T(1024)S(1)}, s32[]{:S(2)}) async-start(f32[1010688]{0:T(1024)} %param.16), calls=%async_computation.2 | async-start | bytes 65536 | tf_op jit(solution)/shard_map/slice | solution.py:50
  52.5 28.0 %copy-start.52 = (f32[64,32,4,4]{0,1,3,2:T(8,128)}, f32[64,32,4,4]{0,1,3,2:T(8,128)S(1)}, u32[]{:S(2)}) copy-start(f32[64,32,4,4]{0,1,3,2:T(8,128)S(1)} %copy.124) | copy-start | bytes 393220
  65.7 21.6 %copy-start.49 = (f32[64,64,3,3]{0,1,3,2:T(8,128)}, f32[64,64,3,3]{0,1,3,2:T(8,128)S(1)}, u32[]{:S(2)}) copy-start(f32[64,64,3,3]{0,1,3,2:T(8,128)S(1)} %copy.153) | copy-start | bytes 442372
  80.4 6.9 %copy-start.3 = (f32[120,32,20,20]{0,1,3,2:T(8,128)}, f32[120,32,20,20]{0,1,3,2:T(8,128)S(1)}, u32[]{:S(2)}) copy-start(f32[120,32,20,20]{0,1,3,2:T(8,128)S(1)} %fusion.221) | copy-start | bytes 18432004
  87.3 6.1 %copy-start.148 = (f32[120,64,9,9]{0,1,3,2:T(8,128)}, f32[120,64,9,9]{0,1,3,2:T(8,128)S(1)}, u32[]{:S(2)}) copy-start(f32[120,64,9,9]{0,1,3,2:T(8,128)S(1)} %fusion.70) | copy-start | bytes 7464964
  94.5 3.6 copy-start.109
  94.5 6.4 %copy-start.80 = (s32[4,30]{1,0:T(4,128)S(1)}, s32[4,30]{1,0:T(4,128)}, u32[]{:S(2)}) copy-start(s32[4,30]{1,0:T(4,128)} %param.13) | copy-start | bytes 1444
  98.0 7.0 %copy-start.29 = (f32[120,128]{1,0:T(8,128)}, f32[120,128]{1,0:T(8,128)S(1)}, u32[]{:S(2)}) copy-start(f32[120,128]{1,0:T(8,128)S(1)} %fusion.32) | copy-start | bytes 184324
  108.2 30.2 %copy-start.7 = (f32[360,128]{1,0:T(8,128)}, f32[360,128]{1,0:T(8,128)S(1)}, u32[]{:S(2)}) copy-start(f32[360,128]{1,0:T(8,128)S(1)} %add.491) | copy-start | bytes 552964
  115.3 17.7 %copy-start.44 = (pred[4,90,90]{1,2,0:T(8,128)(4,1)}, pred[4,90,90]{1,2,0:T(8,128)(4,1)S(1)}, u32[]{:S(2)}) copy-start(pred[4,90,90]{1,2,0:T(8,128)(4,1)S(1)} %broadcast_and_fusion) | copy-start | bytes 97204
  139.9 5.1 copy-start.94
  140.0 5.1 copy-start.74
  141.8 4.2 copy-start.107
  141.8 4.2 copy-start.124
  146.1 7.0 %copy-start.22 = (f32[360,128]{1,0:T(8,128)}, f32[360,128]{1,0:T(8,128)S(1)}, u32[]{:S(2)}) copy-start(f32[360,128]{1,0:T(8,128)S(1)} %multiply_add_fusion.5) | copy-start | bytes 552964
  164.1 5.9 %copy-start.108 = (f32[128]{0:T(128)S(1)}, f32[128]{0:T(128)}, u32[]{:S(2)}) copy-start(f32[128]{0:T(128)} %get-tuple-element.70) | copy-start | bytes 1540
  164.1 5.9 %copy-start.123 = (f32[128]{0:T(128)S(1)}, f32[128]{0:T(128)}, u32[]{:S(2)}) copy-start(f32[128]{0:T(128)} %get-tuple-element.71) | copy-start | bytes 1540
  173.5 5.7 copy-start.37
  182.3 6.6 %copy-start.35 = (f32[360,512]{1,0:T(8,128)S(1)}, f32[360,512]{1,0:T(8,128)}, u32[]{:S(2)}) copy-start(f32[360,512]{1,0:T(8,128)} %copy-done.34) | copy-start | bytes 2211844
  182.3 6.6 %copy-start.63 = (f32[4,1,16384]{2,1,0:T(1,128)S(1)}, f32[4,1,16384]{2,1,0:T(1,128)}, u32[]{:S(2)}) copy-start(f32[4,1,16384]{2,1,0:T(1,128)} %get-tuple-element.91) | copy-start | bytes 786436
  194.0 6.5 %copy-start.9 = (f32[360,128]{1,0:T(8,128)}, f32[360,128]{1,0:T(8,128)S(1)}, u32[]{:S(2)}) copy-start(f32[360,128]{1,0:T(8,128)S(1)} %get-tuple-element.43) | copy-start | bytes 552964
  205.8 3.9 copy-start.6
  205.8 3.9 copy-start.77
  209.5 4.5 copy-start.10
  209.5 5.2 copy-start.33
  238.7 17.3 %slice-start.1 = ((s8[6553600]{0:T(1024)(128)(4,1)}), s8[4194304]{0:T(1024)(128)(4,1)S(1)}, s32[]{:S(2)}) async-start(s8[6553600]{0:T(1024)(128)(4,1)} %bitcast.291), calls=%async_computation.3 | async-start | bytes 8388608
  241.2 6.8 %copy-start.50 = (f32[64,64,3,3]{0,1,3,2:T(8,128)S(1)}, f32[64,64,3,3]{0,1,3,2:T(8,128)}, u32[]{:S(2)}) copy-start(f32[64,64,3,3]{0,1,3,2:T(8,128)} %copy-done.49) | copy-start | bytes 442372
  241.2 14.9 %slice-start.2 = ((s8[6553600]{0:T(1024)(128)(4,1)}), s8[2359296]{0:T(1024)(128)(4,1)S(1)}, s32[]{:S(2)}) async-start(s8[6553600]{0:T(1024)(128)(4,1)} %bitcast.291), calls=%async_computation.4 | async-start | bytes 4718592
  248.0 8.0 %copy-start.147 = (f32[32]{0:T(128)S(1)}, f32[32]{0:T(128)}, u32[]{:S(2)}) copy-start(f32[32]{0:T(128)} %copy-done.146) | copy-start | bytes 388
  256.1 10.1 %copy-start.53 = (f32[64,32,4,4]{0,1,3,2:T(8,128)S(1)}, f32[64,32,4,4]{0,1,3,2:T(8,128)}, u32[]{:S(2)}) copy-start(f32[64,32,4,4]{0,1,3,2:T(8,128)} %copy-done.52) | copy-start | bytes 393220
  266.1 23.8 %copy-start.60 = (f32[512,128]{1,0:T(8,128)S(1)}, f32[512,128]{1,0:T(8,128)}, u32[]{:S(2)}) copy-start(f32[512,128]{1,0:T(8,128)} %fusion.77) | copy-start | bytes 786436
  266.1 23.9 %copy-start.27 = (f32[128,512]{1,0:T(8,128)S(1)}, f32[128,512]{1,0:T(8,128)}, u32[]{:S(2)}) copy-start(f32[128,512]{1,0:T(8,128)} %fusion.90) | copy-start | bytes 786436
  266.1 24.1 %copy-start.55 = (f32[128,128]{1,0:T(8,128)S(1)}, f32[128,128]{1,0:T(8,128)}, u32[]{:S(2)}) copy-start(f32[128,128]{1,0:T(8,128)} %fusion.223) | copy-start | bytes 196612
  309.1 7.4 %copy-start.54 = (f32[64,32,4,4]{0,1,3,2:T(8,128)S(1)}, f32[64,32,4,4]{0,1,3,2:T(8,128)}, u32[]{:S(2)}) copy-start(f32[64,32,4,4]{0,1,3,2:T(8,128)} %fusion.69) | copy-start | bytes 393220
  327.4 23.3 %copy-start.57 = (f32[4,30,128]{2,1,0:T(8,128)S(1)}, f32[4,30,128]{2,1,0:T(8,128)}, u32[]{:S(2)}) copy-start(f32[4,30,128]{2,1,0:T(8,128)} %reduce_sum.596) | copy-start | bytes 184324
  565.5 10.2 %copy-start.24 = (f32[98560]{0:T(1024)S(1)}, f32[98560]{0:T(1024)}, u32[]{:S(2)}) copy-start(f32[98560]{0:T(1024)} %param.19) | copy-start | bytes 1182724
  565.5 10.2 %copy-start.47 = (f32[98560]{0:T(1024)S(1)}, f32[98560]{0:T(1024)}, u32[]{:S(2)}) copy-start(f32[98560]{0:T(1024)} %param.20) | copy-start | bytes 1182724
  565.5 10.2 %copy-start.48 = (f32[98560]{0:T(1024)S(1)}, f32[98560]{0:T(1024)}, u32[]{:S(2)}) copy-start(f32[98560]{0:T(1024)} %param.21) | copy-start | bytes 1182724
  (108 other events, 204.3 us)
Sparse Core Ops, SparseCore 0:
  10.1 22.3 all-gather.2
  403.9 153.3 all-reduce.35

commit v2 on v1

--- a/solution.py
+++ b/solution.py
@@ -4,6 +4,8 @@
 import jax
 import jax.numpy as jnp
 from jax import lax
+from jax.experimental import pallas as pl
+from jax.experimental.pallas import tpu as pltpu
 from jax.sharding import PartitionSpec as P
 
 D = 128
@@ -103,7 +105,7 @@
     return jax.nn.gelu(result + bias[None, :, None, None])
 
 
-def embed_tokens(params, frames, returns, actions, starts):
+def embed_tokens(params, frames, returns, actions, times):
     wins, steps = returns.shape
     images = frames.reshape(wins * steps, 4, 84, 84)
     hidden = conv_layer(images, params["conv_one"], params["bias_one"], 4)
@@ -119,8 +121,6 @@
     rewards = jnp.tanh(returns[:, :, None] * rows[base + 2] + rows[base + 3])
     picks = jax.nn.one_hot(actions, ACT, dtype=jnp.float32)
     moves = jnp.tanh(jnp.einsum("wsa,ad->wsd", picks, params["action_table"], precision=high))
-    places = starts[:, None] + jnp.arange(steps, dtype=jnp.int32)[None, :]
-    times = jnp.take(params["time_table"], places, axis=0)
     tokens = jnp.stack([rewards, states, moves], axis=2) + times[:, :, None, :]
     return tokens.reshape(wins * 3 * steps, D)
 
@@ -185,15 +185,511 @@
     return jnp.sum((total - picked) * valid)
 
 
-def adam_update(weights, first, second, grads):
-    first = beta_first * first + (1 - beta_first) * grads
-    second = beta_second * second + (1 - beta_second) * grads * grads
-    fix_one = 1 - beta_first**STEP
-    fix_two = 1 - beta_second**STEP
-    weights = weights - learn_rate * (
-        first / fix_one / (jnp.sqrt(second / fix_two) + adam_epsilon) + weight_decay * weights
-    )
-    return (weights, first, second)
+def bit_orders(dp_size, mp_size):
+    dp_bits = [("dp", k) for k in range(dp_size.bit_length() - 1)]
+    mp_bits = [("mp", k) for k in range(mp_size.bit_length() - 1)]
+    core, ys = mp_bits[:1], mp_bits[1:]
+    middle = len(dp_bits) // 3
+    xs, zs = dp_bits[:middle], dp_bits[middle:]
+    return [core + xs + zs + ys, core + zs + ys + xs, core + ys + xs + zs]
+
+
+def reduce_kernel(plan, *refs):
+    inputs, steps = plan["inputs"], plan["steps"]
+    ins = refs[: len(inputs)]
+    out_shared, out_split, out_square = refs[len(inputs) : len(inputs) + 3]
+    (work, landing, total, split_total, tiles, tile_in) = refs[len(inputs) + 3 : len(inputs) + 9]
+    (load_sem, send_sem, recv_sem, tile_send, tile_recv, store_sem) = refs[len(inputs) + 9 :]
+    spots = {"dp": lax.axis_index("dp"), "mp": lax.axis_index("mp")}
+
+    def value(bit):
+        return lax.rem(lax.div(spots[bit[0]], 1 << bit[1]), 2)
+
+    def partner(bit):
+        axis, k = bit
+        other = spots[axis] + (1 - 2 * value(bit)) * (1 << k)
+        place = dict(spots)
+        place[axis] = other
+        return (place["dp"], place["mp"])
+
+    loads = []
+    for number, (start, rows) in enumerate(inputs):
+        loads.append(
+            pltpu.make_async_copy(
+                ins[number], work.at[pl.ds(start, rows)], load_sem.at[number]
+            )
+        )
+        loads[-1].start()
+    for start, rows in plan["blank"]:
+        work[pl.ds(start, rows)] = jnp.zeros((rows, 128), jnp.float32)
+    barrier = pltpu.get_barrier_semaphore()
+    bits = plan["bits"]
+    for bit in bits:
+        pl.semaphore_signal(
+            barrier, inc=1, device_id=partner(bit), device_id_type=pl.DeviceIdType.MESH
+        )
+    pl.semaphore_wait(barrier, len(bits))
+    for load in loads:
+        load.wait()
+
+    def add_rows(target, start, source_start, rows):
+        chunk = math.gcd(rows, 64)
+
+        def body(turn, carry):
+            spot = pl.multiple_of(start + turn * chunk, 8)
+            place = pl.multiple_of(source_start + turn * chunk, 8)
+            target[pl.ds(spot, chunk)] = (
+                target[pl.ds(spot, chunk)] + landing[pl.ds(place, chunk)]
+            )
+            return carry
+
+        lax.fori_loop(0, rows // chunk, body, 0)
+
+    streams = plan["streams"]
+    where = [stream["base"] for stream in streams]
+    sizes = [stream["rows"] for stream in streams]
+    flights = [None] * len(streams)
+    landings = [stream["landing"] for stream in streams]
+    slot = 0
+    for step in range(steps):
+        for number, stream in enumerate(streams):
+            if flights[number] is not None:
+                copy, half, land, keep = flights[number]
+                copy.wait()
+                add_rows(work, keep, land, half)
+                where[number] = keep
+            bit = stream["order"][step]
+            half = sizes[number] // 2
+            mine = value(bit)
+            keep = where[number] + mine * half
+            give = where[number] + (1 - mine) * half
+            copy = pltpu.make_async_remote_copy(
+                src_ref=work.at[pl.ds(pl.multiple_of(give, 8), half)],
+                dst_ref=landing.at[pl.ds(landings[number], half)],
+                send_sem=send_sem.at[slot],
+                recv_sem=recv_sem.at[slot],
+                device_id=partner(bit),
+                device_id_type=pl.DeviceIdType.MESH,
+            )
+            copy.start()
+            slot += 1
+            flights[number] = (copy, half, landings[number], keep)
+            landings[number] += half
+            sizes[number] = half
+    backs = [list(reversed(stream["order"][stream["shared"] :])) for stream in streams]
+    spaces = []
+    for number, stream in enumerate(streams):
+        copy, half, land, keep = flights[number]
+        copy.wait()
+        add_rows(work, keep, land, half)
+        where[number] = keep
+        if stream["shared"]:
+            spaces.append(split_total)
+            low = keep
+            for bit in stream["order"][: stream["shared"]]:
+                pass
+            rows = half
+            offset = jnp.int32(0)
+            size = stream["rows"] >> stream["shared"]
+            for bit in stream["order"][stream["shared"] :]:
+                size //= 2
+                offset = offset + value(bit) * size
+            split_total[pl.ds(pl.multiple_of(offset, 8), rows)] = work[
+                pl.ds(pl.multiple_of(keep, 8), rows)
+            ]
+            held = work[pl.ds(pl.multiple_of(keep, 8), rows)]
+            squares = held * held
+            tiles[0] = jnp.sum(squares.reshape(rows // 8, 8, 128), axis=0)
+            where[number] = offset
+        else:
+            spaces.append(total)
+            total[pl.ds(pl.multiple_of(keep, 8), half)] = work[
+                pl.ds(pl.multiple_of(keep, 8), half)
+            ]
+    flights = [None] * len(streams)
+    tile_flight = None
+    for step in range(steps):
+        if tile_flight is not None:
+            tile_flight.wait()
+            tiles[step] = tiles[step - 1] + tile_in[step - 1]
+        tile_flight = pltpu.make_async_remote_copy(
+            src_ref=tiles.at[step],
+            dst_ref=tile_in.at[step],
+            send_sem=tile_send.at[step],
+            recv_sem=tile_recv.at[step],
+            device_id=partner(bits[step]),
+            device_id_type=pl.DeviceIdType.MESH,
+        )
+        tile_flight.start()
+        for number, stream in enumerate(streams):
+            if flights[number] is not None:
+                copy, low, size = flights[number]
+                copy.wait()
+                where[number] = low
+                sizes[number] = size
+                flights[number] = None
+            if step >= len(backs[number]):
+                continue
+            bit = backs[number][step]
+            rows = sizes[number]
+            region = spaces[number].at[pl.ds(pl.multiple_of(where[number], 8), rows)]
+            copy = pltpu.make_async_remote_copy(
+                src_ref=region,
+                dst_ref=region,
+                send_sem=send_sem.at[slot],
+                recv_sem=recv_sem.at[slot],
+                device_id=partner(bit),
+                device_id_type=pl.DeviceIdType.MESH,
+            )
+            copy.start()
+            slot += 1
+            flights[number] = (copy, where[number] - value(bit) * rows, rows * 2)
+    tile_flight.wait()
+    out_square[...] = tiles[steps - 1] + tile_in[steps - 1]
+    stores = []
+    for number, stream in enumerate(streams):
+        if flights[number] is not None:
+            flights[number][0].wait()
+    shared_rows = total.shape[0]
+    stores.append(
+        pltpu.make_async_copy(total, out_shared.at[pl.ds(0, shared_rows)], store_sem.at[0])
+    )
+    stores.append(pltpu.make_async_copy(split_total, out_split, store_sem.at[1]))
+    for store in stores:
+        store.start()
+    for store in stores:
+        store.wait()
+
+
+def reduce_all(pieces, split_blocks, dp_size, mp_size, out_rows, collective_id):
+    orders = bit_orders(dp_size, mp_size)
+    bits = orders[0]
+    steps = len(bits)
+    grain = 8 << steps
+    used = max(start + array.shape[0] for start, array in pieces)
+    half = -(-used // (2 * grain)) * grain
+    shared_rows = 2 * half
+    span = split_blocks[0].shape[0]
+    split_grain = 8 * dp_size
+    block = -(-span // split_grain) * split_grain
+    inputs, arrays, blank = [], [], []
+    reach = 0
+    for start, array in pieces:
+        if start > reach:
+            blank.append((reach, start - reach))
+        inputs.append((start, array.shape[0]))
+        arrays.append(array)
+        reach = start + array.shape[0]
+    if shared_rows > reach:
+        blank.append((reach, shared_rows - reach))
+    shared_steps = mp_size.bit_length() - 1
+    for number in range(mp_size):
+        turned = 0
+        for k in range(shared_steps):
+            turned |= ((number >> k) & 1) << (shared_steps - 1 - k)
+        start = shared_rows + turned * block
+        inputs.append((start, span))
+        arrays.append(split_blocks[number])
+        if block > span:
+            blank.append((start + span, block - span))
+    split_rows = mp_size * block
+    work_rows = shared_rows + split_rows
+    streams = [
+        dict(base=0, rows=half, order=orders[0], shared=0, landing=0),
+        dict(base=half, rows=half, order=orders[1], shared=0, landing=half),
+        dict(
+            base=shared_rows,
+            rows=split_rows,
+            order=orders[2],
+            shared=shared_steps,
+            landing=shared_rows,
+        ),
+    ]
+    plan = dict(inputs=inputs, blank=blank, streams=streams, bits=bits, steps=steps)
+    copies = 3 * 2 * steps
+    return pl.pallas_call(
+        partial(reduce_kernel, plan),
+        out_shape=(
+            jax.ShapeDtypeStruct((out_rows, 128), jnp.float32),
+            jax.ShapeDtypeStruct((block, 128), jnp.float32),
+            jax.ShapeDtypeStruct((8, 128), jnp.float32),
+        ),
+        in_specs=[pl.BlockSpec(memory_space=pl.ANY)] * len(arrays),
+        out_specs=(
+            pl.BlockSpec(memory_space=pl.ANY),
+            pl.BlockSpec(memory_space=pl.ANY),
+            pl.BlockSpec(memory_space=pltpu.VMEM),
+        ),
+        scratch_shapes=[
+            pltpu.VMEM((work_rows, 128), jnp.float32),
+            pltpu.VMEM((work_rows, 128), jnp.float32),
+            pltpu.VMEM((shared_rows, 128), jnp.float32),
+            pltpu.VMEM((block, 128), jnp.float32),
+            pltpu.VMEM((steps, 8, 128), jnp.float32),
+            pltpu.VMEM((steps, 8, 128), jnp.float32),
+            pltpu.SemaphoreType.DMA((len(arrays),)),
+            pltpu.SemaphoreType.DMA((copies,)),
+            pltpu.SemaphoreType.DMA((copies,)),
+            pltpu.SemaphoreType.DMA((steps,)),
+            pltpu.SemaphoreType.DMA((steps,)),
+            pltpu.SemaphoreType.DMA((2,)),
+        ],
+        compiler_params=pltpu.CompilerParams(
+            collective_id=collective_id,
+            has_side_effects=True,
+            vmem_limit_bytes=56 * 1024 * 1024,
+        ),
+        name="reduce_gradients",
+    )(*arrays)
+
+
+def spans(fast_rows):
+    places = {}
+    at = 0
+    for name, rows in [
+        ("encoder", 3136),
+        ("conv", 616),
+        ("vectors", 24),
+        ("action_table", 24),
+        ("head", 24),
+        ("scalars", 8),
+        ("times", fast_rows),
+    ]:
+        places[name] = (at, rows)
+        at += rows
+    return places, at
+
+
+FLAT_ROWS = 7896
+BLOCK_ROWS = 512
+LATE = 609
+
+
+def adam_kernel(
+    fast_rows,
+    most_rows,
+    starts_ref,
+    lengths_ref,
+    flag_ref,
+    reduced_ref,
+    split_ref,
+    square_ref,
+    weight_ref,
+    first_ref,
+    second_ref,
+    split_weight_ref,
+    split_first_ref,
+    split_second_ref,
+    new_ref,
+    new_first_ref,
+    new_second_ref,
+    split_new_ref,
+    split_new_first_ref,
+    split_new_second_ref,
+    scalar_ref,
+    pulled,
+    flat,
+    factor_ref,
+    edge_ref,
+    pull_sem,
+):
+    step = pl.program_id(0)
+    places, fast_total = spans(fast_rows)
+    lane = lax.broadcasted_iota(jnp.int32, (1, 128), 1)
+
+    def update(weights, first, second, grads):
+        first = beta_first * first + (1 - beta_first) * grads
+        second = beta_second * second + (1 - beta_second) * grads * grads
+        fix_one = 1 - beta_first**STEP
+        fix_two = 1 - beta_second**STEP
+        weights = weights - learn_rate * (
+            first / fix_one / (jnp.sqrt(second / fix_two) + adam_epsilon) + weight_decay * weights
+        )
+        return weights, first, second
+
+    @pl.when(step == 0)
+    def prepare():
+        pull = pltpu.make_async_copy(
+            reduced_ref.at[pl.ds(0, fast_total)], pulled.at[pl.ds(0, fast_total)], pull_sem
+        )
+        pull.start()
+        times_at = LATE + 35
+        table_at = LATE + 17 + ACT
+
+        def wipe(turn, carry):
+            flat[pl.ds(pl.multiple_of(turn * 64, 64), 64)] = jnp.zeros((64, 128), jnp.float32)
+            return carry
+
+        lax.fori_loop(0, flat.shape[0] // 64, wipe, 0)
+        pull.wait()
+        squares = jnp.zeros((8, 128), jnp.float32)
+
+        def fold(rows):
+            return jnp.sum((rows * rows).reshape(-1, 8, 128), axis=0)
+
+        def conv_rows(turn, carry):
+            spot = pl.multiple_of(turn * 56, 8)
+            held = pulled[pl.ds(places["conv"][0] + spot, 56)]
+            flat[pl.ds(8 + spot, 56)] = held
+            return carry + fold(held)
+
+        squares = lax.fori_loop(0, 616 // 56, conv_rows, squares)
+        edge_ref[...] = flat[LATE : LATE + 16]
+
+        def encoder_rows(turn, carry):
+            spot = pl.multiple_of(turn * 64, 64)
+            held = pulled[pl.ds(spot, 64)]
+            flat[pl.ds(8 + LATE + spot, 64)] = pltpu.roll(held, 32, 1)
+            return carry + fold(held)
+
+        squares = lax.fori_loop(0, 3136 // 64, encoder_rows, squares)
+        for name, at, rows in [
+            ("vectors", LATE + 3136, 17),
+            ("action_table", LATE + 3153, ACT),
+            ("head", LATE + 3171 + TSTEPS, ACT),
+        ]:
+            held = pulled[places[name][0] : places[name][0] + 24]
+            squares = squares + fold(held)
+            flat[8 + at : 8 + at + rows] = pltpu.roll(held, 32, 1)[:rows]
+        time_at = 8 + LATE + 3171
+
+        @pl.when(flag_ref[0] > 0)
+        def scatter():
+            windows = starts_ref.shape[0]
+
+            def window(number, offset):
+                length = lengths_ref[number]
+                start = starts_ref[number]
+
+                def chunk(turn, carry):
+                    rows = pulled[pl.ds(places["times"][0] + offset + turn * 8, 8)]
+                    left = length - turn * 8
+                    keep = lax.broadcasted_iota(jnp.int32, (8, 1), 0) < left
+                    spot = pl.ds(time_at + start + turn * 8, 8)
+                    flat[spot] = flat[spot] + jnp.where(keep, pltpu.roll(rows, 32, 1), 0.0)
+                    return carry
+
+                lax.fori_loop(0, lax.div(length + 7, 8), chunk, 0)
+                return offset + length
+
+            lax.fori_loop(0, windows, window, jnp.int32(0))
+
+        @pl.when(flag_ref[0] <= 0)
+        def whole_table():
+            pull_table = pltpu.make_async_copy(
+                reduced_ref.at[pl.ds(places["times"][0], TSTEPS)],
+                pulled.at[pl.ds(places["times"][0], TSTEPS)],
+                pull_sem,
+            )
+            pull_table.start()
+            pull_table.wait()
+
+            def rows_in(turn, carry):
+                spot = pl.multiple_of(turn * 64, 64)
+                held = pulled[pl.ds(places["times"][0] + spot, 64)]
+                flat[pl.ds(time_at + spot, 64)] = pltpu.roll(held, 32, 1)
+                return carry
+
+            lax.fori_loop(0, TSTEPS // 64, rows_in, 0)
+
+        def time_squares(turn, carry):
+            return carry + fold(flat[pl.ds(time_at + turn * 64, 64)])
+
+        squares = lax.fori_loop(0, TSTEPS // 64, time_squares, squares)
+        squares = squares + square_ref[...]
+        count = jnp.float32(0)
+        whole = lax.fori_loop(
+            0, lengths_ref.shape[0], lambda k, c: c + lengths_ref[k], jnp.int32(0)
+        )
+        count = jnp.full((1, 128), whole.astype(jnp.float32))
+        scalars = pulled[places["scalars"][0] : places["scalars"][0] + 8]
+        total = jnp.sum(jnp.sum(squares, axis=0, keepdims=True), axis=1, keepdims=True)
+        seed = 1.0 / count
+        norm = jnp.sqrt(jnp.broadcast_to(total, (1, 128))) * seed
+        factor = jnp.minimum(1.0, clip_limit / (norm + 1e-06)) * seed
+        factor_ref[...] = jnp.broadcast_to(factor, (8, 128))
+        loss = jnp.broadcast_to(scalars[0:1, 0:1], (1, 128))
+        row = lax.broadcasted_iota(jnp.int32, (8, 128), 0)
+        scalar_ref[...] = jnp.where(row == 0, norm, jnp.where(row == 1, loss, count))
+        split_rows = split_weight_ref.shape[0]
+        outs = update(
+            split_weight_ref[...],
+            split_first_ref[...],
+            split_second_ref[...],
+            split_ref[0:split_rows] * factor,
+        )
+        split_new_ref[...], split_new_first_ref[...], split_new_second_ref[...] = outs
+
+    base = pl.multiple_of(step * BLOCK_ROWS, BLOCK_ROWS)
+    factor = factor_ref[0:1]
+    own = flat[pl.ds(8 + base, BLOCK_ROWS)]
+    before = flat[pl.ds(7 + base, BLOCK_ROWS)]
+    row = lax.broadcasted_iota(jnp.int32, (BLOCK_ROWS, 1), 0) + base
+    late = row >= LATE
+    before = jnp.where(row == LATE, edge_ref[8:9], before)
+    grads = jnp.where(late & (lane < 32), before, own)
+    outs = update(weight_ref[...], first_ref[...], second_ref[...], grads * factor)
+    new_ref[...], new_first_ref[...], new_second_ref[...] = outs
+
+
+def adam_all(
+    starts, lengths, flag, reduced, split_grad, square, shared, split, fast_rows
+):
+    places, fast_total = spans(fast_rows)
+    most = places["times"][0] + TSTEPS
+    grid = -(-FLAT_ROWS // BLOCK_ROWS)
+    flat_spec = pl.BlockSpec((BLOCK_ROWS, 128), lambda i, *_: (i, 0))
+    split_rows = split[0].shape[0]
+
+    def whole(shape):
+        return pl.BlockSpec(shape, lambda i, *_: (0,) * len(shape))
+
+    split_spec = whole((split_rows, 128))
+    shared_out = jax.ShapeDtypeStruct((FLAT_ROWS, 128), jnp.float32)
+    split_out = jax.ShapeDtypeStruct((split_rows, 128), jnp.float32)
+    return pl.pallas_call(
+        partial(adam_kernel, fast_rows, most),
+        grid_spec=pltpu.PrefetchScalarGridSpec(
+            num_scalar_prefetch=3,
+            grid=(grid,),
+            in_specs=[
+                pl.BlockSpec(memory_space=pl.ANY),
+                whole(split_grad.shape),
+                whole((8, 128)),
+                flat_spec,
+                flat_spec,
+                flat_spec,
+                split_spec,
+                split_spec,
+                split_spec,
+            ],
+            out_specs=[flat_spec] * 3 + [split_spec] * 3 + [whole((8, 128))],
+            scratch_shapes=[
+                pltpu.VMEM((most, 128), jnp.float32),
+                pltpu.VMEM((grid * BLOCK_ROWS + 64, 128), jnp.float32),
+                pltpu.VMEM((8, 128), jnp.float32),
+                pltpu.VMEM((16, 128), jnp.float32),
+                pltpu.SemaphoreType.DMA,
+            ],
+        ),
+        out_shape=[shared_out] * 3
+        + [split_out] * 3
+        + [jax.ShapeDtypeStruct((8, 128), jnp.float32)],
+        compiler_params=pltpu.CompilerParams(vmem_limit_bytes=48 * 1024 * 1024),
+        name="adam_update",
+    )(starts, lengths, flag, reduced, split_grad, square, *shared, *split)
+
+
+def valid_slots(lengths, steps, room):
+    ends = jnp.cumsum(lengths)
+    slot = jnp.arange(room, dtype=jnp.int32)
+    window = jnp.sum((slot[:, None] >= ends[None, :]).astype(jnp.int32), axis=1)
+    window = jnp.minimum(window, lengths.shape[0] - 1)
+    begin = (ends - lengths)[window]
+    return window, jnp.minimum(slot - begin, steps - 1), ends[-1]
+
+
+FAST_ROWS = 776
 
 
 def per_device(
@@ -209,16 +705,24 @@
     split_first,
     split_second,
 ):
-    parts = lax.axis_size("mp")
-    narrow = D // parts
-    hidden_width = FF // parts
+    dp_size, mp_size = lax.axis_size("dp"), lax.axis_size("mp")
+    narrow = D // mp_size
+    hidden_width = FF // mp_size
+    wins, steps = returns.shape
+    room = 128
     split_all = lax.all_gather(split_weights, "mp", axis=0, tiled=True)
+    index_own = jnp.concatenate([starts, lengths]).astype(jnp.float32)
+    index_all = lax.all_gather(index_own, ("dp", "mp"), axis=0).astype(jnp.int32)
+    starts_all = index_all[:, :wins].reshape(-1)
+    lengths_all = index_all[:, wins:].reshape(-1)
     params = unpack_shared(shared_weights)
     images = frames.astype(jnp.float32)
-
-    def local_loss(table, flat):
-        layers = assemble(flat, parts, narrow, hidden_width)
-        stream = embed_tokens(table, images, returns, actions, starts)
+    places = starts[:, None] + jnp.arange(steps, dtype=jnp.int32)[None, :]
+    times = jnp.take(params["time_table"], places, axis=0)
+
+    def local_loss(table, flat, times):
+        layers = assemble(flat, mp_size, narrow, hidden_width)
+        stream = embed_tokens(table, images, returns, actions, times)
         for layer in range(LAYERS):
             weights = layers[layer]
             normed = first_piece(stream, table["vectors"], layer)
@@ -228,43 +732,90 @@
             stream = last_piece(stream, mixed, table["vectors"], layer)
         return action_loss(stream, table, actions, lengths)
 
-    loss_local, (grads, split_grad) = jax.value_and_grad(local_loss, argnums=(0, 1))(
-        params, split_all
-    )
-    count_local = jnp.sum(lengths).astype(jnp.float32)
-    pieces = [grads[name].reshape(-1) for name, shape in shared_layout()]
-    raw = sum(piece.shape[0] for piece in pieces)
-    total = shared_weights.shape[0]
-    tail = jnp.zeros((total - raw,), jnp.float32)
-    scalars = jnp.stack([loss_local, count_local])
-    flat = jnp.concatenate(pieces + [tail, split_grad, scalars])
-    summed = lax.psum(flat, ("dp", "mp"))
-    loss_sum = summed[-2]
-    valid_count = summed[-1]
-    seed = 1.0 / valid_count
-    summed = summed[:-2] * seed
-    grad_norm = jnp.sqrt(jnp.sum(summed * summed))
-    factor = jnp.minimum(1.0, clip_limit / (grad_norm + 1e-06))
+    loss_local, (grads, split_grad, time_grad) = jax.value_and_grad(local_loss, argnums=(0, 1, 2))(
+        params, split_all, times
+    )
+
+    def padded(flat, rows):
+        return jnp.pad(flat.reshape(-1), (0, rows * 128 - flat.size)).reshape(rows, 128)
+
+    conv_names = ["conv_one", "bias_one", "conv_two", "bias_two", "conv_three", "bias_three"]
+    conv_flat = jnp.concatenate([grads[name].reshape(-1) for name in conv_names])
+    small = jnp.concatenate(
+        [
+            padded(conv_flat, 616),
+            padded(grads["vectors"], 24),
+            padded(grads["action_table"], 24),
+            padded(grads["head"], 24),
+            jnp.broadcast_to(loss_local, (8, 128)),
+        ]
+    )
     width = split_weights.shape[0]
-    split_sum = lax.dynamic_slice(summed, (total + lax.axis_index("mp") * width,), (width,))
-    split_new, split_m, split_v = adam_update(
-        split_weights, split_first, split_second, split_sum * factor
-    )
-    shared_new, shared_m, shared_v = adam_update(
-        shared_weights, shared_first, shared_second, summed[:total] * factor
-    )
+    split_rows = -(-width // 128)
+    split_pad = -(-split_rows // 8) * 8
+    split_blocks = [
+        padded(split_grad[number * width : (number + 1) * width], split_pad)
+        for number in range(mp_size)
+    ]
+    window, moment, used = valid_slots(lengths, steps, room)
+    slot = jnp.arange(room, dtype=jnp.int32)
+    packed = time_grad.reshape(wins * steps, D)[window * steps + moment]
+    packed = jnp.where((slot < used)[:, None], packed, 0.0)
+    spots, fast_total = spans(FAST_ROWS)
+    out_rows = spots["times"][0] + TSTEPS
+    out_rows = -(-out_rows // 4096) * 4096
+    rows_all = jnp.sum(lengths_all)
+    fast = rows_all <= FAST_ROWS
+    me = lax.axis_index("dp") * mp_size + lax.axis_index("mp")
+    skipped = jnp.sum(
+        jnp.where(jnp.arange(lengths_all.shape[0]) < me * wins, lengths_all, 0)
+    )
+
+    def compact(operands):
+        encoder, small, packed, blocks = operands
+        field = jnp.zeros((FAST_ROWS + room, D), jnp.float32)
+        field = lax.dynamic_update_slice(field, packed, (jnp.minimum(skipped, FAST_ROWS), 0))
+        pieces = [(0, encoder), (3136, small), (spots["times"][0], field[:FAST_ROWS])]
+        return reduce_all(pieces, blocks, dp_size, mp_size, out_rows, 1)
+
+    def whole(operands):
+        encoder, small, packed, blocks = operands
+        spot = starts[window] + moment
+        field = jnp.zeros((TSTEPS, D), jnp.float32).at[spot].add(packed)
+        pieces = [(0, encoder), (3136, small), (spots["times"][0], field)]
+        return reduce_all(pieces, blocks, dp_size, mp_size, out_rows, 2)
+
+    reduced, split_sum, square = lax.cond(
+        fast, compact, whole, (grads["encoder"], small, packed, split_blocks)
+    )
+
+    def rows_of(flat):
+        return padded(flat, split_rows) if width % 128 else flat.reshape(split_rows, 128)
+
+    shared_view = [a.reshape(FLAT_ROWS, 128) for a in (shared_weights, shared_first, shared_second)]
+    split_view = [rows_of(a) for a in (split_weights, split_first, split_second)]
+    results = adam_all(
+        starts_all,
+        lengths_all,
+        fast.astype(jnp.int32).reshape(1),
+        reduced,
+        split_sum,
+        square,
+        shared_view,
+        split_view,
+        FAST_ROWS,
+    )
+    shared_out = [a.reshape(-1) for a in results[:3]]
+    split_out = [a.reshape(-1)[:width] for a in results[3:6]]
+    scalars = results[6]
     return (
-        shared_new,
-        shared_m,
-        shared_v,
-        shared_new.astype(jnp.bfloat16),
-        split_new,
-        split_m,
-        split_v,
-        split_new.astype(jnp.bfloat16),
-        grad_norm,
-        loss_sum,
-        valid_count,
+        *shared_out,
+        shared_out[0].astype(jnp.bfloat16),
+        *split_out,
+        split_out[0].astype(jnp.bfloat16),
+        scalars[0, 0],
+        scalars[1, 0],
+        scalars[2, 0],
     )
 
 

time: 598 us -> 519 us (0.87)
  waiting for transfers between devices: 154 us -> 0.04 us
  Pallas kernels: 0 us -> 91.8 us
  blocking collectives: 0 us -> 51.8 us
  local copies, waits for them, and re-layouts: 201 us -> 158 us
  other arithmetic: 50.1 us -> 36.4 us
  matrix products: 162 us -> 153 us
    psum x1 -> x0, waiting for transfers between devices: 153 us -> none  [per_device(): summed = lax.psum(flat, ('dp', 'mp'))]
    pallas_call x0 -> x2, Pallas kernels: none -> 91.8 us  [the longest x1 58.7 us: reduce_all(): pl.pallas_call(partial(reduce_kernel, plan), out_shape=(jax.ShapeDtypeStr...]
    all_gather x0 -> x1, blocking collectives: none -> 51.8 us  [per_device(): lax.all_gather(index_own, ('dp', 'mp'), axis=0).astype(jnp.int32)]
    concatenate x1 -> x2, local copies, waits for them, and re-layouts: 51 us -> 2.47 us  [the longest x1 1.82 us: per_device(): jnp.concatenate([grads[name].reshape(-1) for name in conv_names])]
    convert_element_type x2 -> x3, other arithmetic: 12.6 us -> 4.39 us  [the longest x1 3.68 us: per_device(): shared_out[0].astype(jnp.bfloat16)]
    slice x1 -> x8, local copies, waits for them, and re-layouts: 1.33 us -> 9.28 us  [the longest x5 6.41 us: per_device(): split_grad[number * width:(number + 1) * width]]
    reshape x4 -> x11, local copies, waits for them, and re-layouts: 13.9 us -> 16.5 us  [the longest x3 13.8 us: per_device(): grads[name].reshape(-1)]
  transfers between devices with their start and end apart: 2 -> 1, of which waited for: 1 -> 0; matrix products, arithmetic and copies ran while one was open for 18% -> 22% of each run, Pallas kernels for 0% -> 0%
where the time goes in v2:
time: 519 us; the launch traced here: 509 us
  local copies, waits for them, and re-layouts  158 us (30%)
  matrix products  153 us (29%)
  Pallas kernels  91.8 us (18%)
  blocking collectives  51.8 us (10%)
  other arithmetic  36.4 us (7%)
  between operations  17.7 us (3%)
    conv_general_dilated x8, matrix products, conv_layer(): lax.conv_general_dilated(images, kernel, (stride, stride), 'VALID', dimen...  96.6 us
    pallas_call x1, Pallas kernels, reduce_all(): pl.pallas_call(partial(reduce_kernel, plan), out_shape=(jax.ShapeDtypeStr...  58.7 us
    all_gather x1, blocking collectives, per_device(): lax.all_gather(index_own, ('dp', 'mp'), axis=0).astype(jnp.int32)  51.8 us
    pallas_call x1, Pallas kernels, adam_all(): pl.pallas_call(partial(adam_kernel, fast_rows, most), grid_spec=pltpu.Pre...  33.2 us
    reshape x8, local copies, waits for them, and re-layouts, unpack_shared(): params[name] = flat[offset:offset + count].reshape(shape)  29.3 us
    reshape x1, local copies, waits for them, and re-layouts, embed_tokens(): images = frames.reshape(wins * steps, 4, 84, 84)  21.8 us
    reshape x3, local copies, waits for them, and re-layouts, per_device(): grads[name].reshape(-1)  13.8 us
    conv_general_dilated x3, local copies, waits for them, and re-layouts, conv_layer(): lax.conv_general_dilated(images, kernel, (stride, stride), 'VALID', dimen...  13.3 us
  transfers between devices with their start and end apart: 1, of which 0 were waited for; matrix products, arithmetic and copies ran while one was open for 22% of the time, Pallas kernels for 0%

profile of v2, /device:TPU:0, one launch (start us, length us, event | category | flops | bytes accessed | tf_op | source)
XLA Modules:
  0.0 509.3 jit_solution(3650351504887881292)
XLA Ops:
  7.2 2.0 reshape.1082
  14.6 3.7 slice_bitcast_fusion
  18.5 21.8 %copy.167 = bf16[120,4,84,84]{0,1,3,2:T(4,128)(2,1)} copy(bf16[120,4,84,84]{3,1,2,0:T(4,128)(2,1)} %bitcast.352) | data formatting | bytes 13547520 | tf_op jit(solution)/shard_map/jvp()/reshape | solution.py:110
  40.9 6.7 %reshape.944 = f32[64,32,4,4]{3,2,1,0:T(4,128)} reshape(f32[32768]{0:T(1024)S(1)} %slice.228) | data formatting | bytes 262144 | tf_op jit(solution)/shard_map/reshape | solution.py:52
  47.6 4.2 copy.169
  51.8 5.9 %reshape.945 = f32[64,64,3,3]{3,2,1,0:T(4,128)} reshape(f32[36864]{0:T(1024)S(1)} %slice.230) | data formatting | bytes 294912 | tf_op jit(solution)/shard_map/reshape | solution.py:52
  57.8 7.4 %copy.198 = f32[64,64,3,3]{0,1,3,2:T(8,128)S(1)} copy(f32[64,64,3,3]{3,2,1,0:T(4,128)} %reshape.945) | data formatting | bytes 294912 | tf_op jit(solution)/shard_map/reshape | solution.py:52
  65.1 14.5 %fusion.221 = f32[120,32,20,20]{0,1,3,2:T(8,128)S(1)} fusion(bf16[120,4,84,84]{0,1,3,2:T(4,128)(2,1)} %copy.167, f32[32,4,8,8]{0,1,3,2:T(4,128)S(1)} %copy.168), kind=kOutput, calls=%fused_computation.394 | convolution fusion | flops 2359296000 | bytes 12950528 | tf_op jit(solution)/shard_map/jvp()/conv_general_dilated | solution.py:97
  79.6 6.9 %fusion.70 = f32[120,64,9,9]{0,1,3,2:T(8,128)S(1)} fusion(f32[64,32,4,4]{0,1,3,2:T(8,128)S(1)} %copy.169, f32[120,32,20,20]{0,1,3,2:T(8,128)S(1)} %fusion.221, f32[32]{0:T(128)S(1)} %slice.227), kind=kOutput, calls=%fused_computation.128 | convolution fusion | flops 1924853760 | bytes 8763520 | tf_op jit(solution)/shard_map/jvp()/conv_general_dilated | solution.py:97
  86.6 6.0 %multiply_multiply_fusion.8 = (f32[120,64,7,7]{0,1,3,2:T(8,128)S(1)}, f32[120,64,7,7]{0,1,3,2:T(8,128)}) fusion(f32[64]{0:T(128)S(1)} %get-tuple-element.285, f32[64,64,3,3]{0,1,3,2:T(8,128)S(1)} %copy.198, f32[120,64,9,9]{0,1,3,2:T(8,128)S(1)} %fusion.70, f32[64]{0:T(128)S(1)} %get-tuple-element.284), kind=kOutput, calls=%fused_computation.57 | convolution fusion | flops 1309547520 | bytes 5646848 | tf_op jit(solution)/shard_map/jvp()/conv_general_dilated | solution.py:97
  92.6 2.2 copy.171
  96.3 3.4 fusion.34
  101.8 3.2 fusion.139
  105.6 2.2 gather_fusion
  109.0 3.1 slice.232
  116.0 2.6 dot_general.202
  118.7 51.8 %all-gather = f32[32,1,8]{2,1,0:T(1,128)S(1)} all-gather(f32[1,1,8]{2,1,0:T(1,128)S(1)} %fusion.140), channel_id=1, replica_groups=mesh['dp'=8,'mp'=4] {'dp','mp'}, dimensions={0}, use_global_device_ids=true | all-gather | bytes 1056 | tf_op jit(solution)/shard_map/all_gather | solution.py:715
  173.5 6.7 %reduce.5 = f32[4,98560]{1,0:T(4,128)} reduce(f32[4,1,98560]{2,1,0:T(1,128)} %all-gather.4.cloned.1.call-done, f32[]{:T(128)} %constant.244), dimensions={1}, to_apply=%all-gather.1.reduce_sub_computation | reduce | bytes 3153924 | tf_op jit(solution)/shard_map/all_gather | solution.py:713
  180.2 3.8 reshape.951
  184.0 2.9 slice_reduce_fusion.4
  186.9 1.7 fusion.205
  188.6 3.6 fusion.203
  223.4 1.8 multiply_reduce_fusion.7
  227.1 2.7 fusion.76
  236.6 2.9 convolution_bitcast_fusion.7
  239.5 1.9 convert_reduce_fusion.1
  258.0 2.9 convolution_bitcast_fusion.4
  260.9 1.9 convert_reduce_fusion
  272.5 4.0 fusion.218
  276.6 7.1 %fusion.77 = f32[64,64,3,3]{0,1,3,2:T(8,128)} fusion(f32[120,64,7,7]{0,1,3,2:T(8,128)S(1)} %get-tuple-element.344, f32[120,64,9,9]{0,1,3,2:T(8,128)S(1)} %copy-done.145, f32[64]{0:T(128)S(1)} %copy-done.141), kind=kOutput, calls=%fused_computation.142 | convolution fusion | flops 1306160640 | bytes 4141312 | tf_op jit(solution)/shard_map/transpose(jvp())/conv_general_dilated | solution.py:97
  283.7 7.1 %fusion.217 = (f32[64]{0:T(128)S(1)}, f32[120,64,9,9]{0,1,3,2:T(8,128)S(1)}) fusion(f32[120,64,9,9]{0,1,3,2:T(8,128)S(1)} %copy-done.145, f32[64]{0:T(128)S(1)} %copy-done.141, f32[120,64,7,7]{0,1,3,2:T(8,128)S(1)} %get-tuple-element.344, f32[64,64,3,3]{0,1,3,2:T(8,128)S(1)} %copy-done.48), kind=kOutput, calls=%fused_computation.390 | convolution fusion | flops 1313625600 | bytes 6629888 | tf_op jit(solution)/shard_map/transpose(jvp())/conv_general_dilated | solution.py:97
  290.8 10.2 %fusion.69 = f32[64,32,4,4]{0,1,3,2:T(8,128)} fusion(f32[120,64,9,9]{0,1,3,2:T(8,128)S(1)} %get-tuple-element.342, f32[120,32,20,20]{0,1,3,2:T(8,128)S(1)} %bitcast.351, f32[32]{0:T(128)S(1)} %copy-done.143), kind=kOutput, calls=%fused_computation.127 | convolution fusion | flops 1924853760 | bytes 8763520 | tf_op jit(solution)/shard_map/transpose(jvp())/conv_general_dilated | solution.py:97
  301.1 22.5 %fusion.216 = (f32[32]{0:T(128)S(1)}, f32[120,32,20,20]{0,1,3,2:T(8,128)}) fusion(f32[120,32,20,20]{0,1,3,2:T(8,128)S(1)} %bitcast.351, f32[32]{0:T(128)S(1)} %copy-done.143, f32[120,64,9,9]{0,1,3,2:T(8,128)S(1)} %get-tuple-element.342, f32[64,32,4,4]{0,1,3,2:T(8,128)S(1)} %copy-done.52), kind=kOutput, calls=%fused_computation.389 | convolution fusion | flops 1943285760 | bytes 14907648 | tf_op jit(solution)/shard_map/transpose(jvp())/conv_general_dilated | solution.py:97
  323.6 1.9 fusion.187
  332.0 2.8 pad_add_fusion
  334.9 5.1 %slice_reduce_fusion = (f32[2,49280]{1,0:T(2,128)S(1)}, f32[2,49280]{1,0:T(2,128)S(1)}, f32[2,49280]{1,0:T(2,128)S(1)}, f32[2,49280]{1,0:T(2,128)S(1)}) fusion(f32[4,2,49280]{2,0,1:T(4,128)S(1)} %pad_add_fusion), kind=kLoop, calls=%fused_computation.135 | loop fusion | bytes 3153920 | tf_op jit(solution)/shard_map/slice | solution.py:757
  344.0 8.2 %copy.203 = f32[64,64,3,3]{3,2,1,0:T(4,128)} copy(f32[64,64,3,3]{0,1,3,2:T(8,128)S(1)} %copy-done.49) | data formatting | bytes 294912 | tf_op jit(solution)/shard_map/transpose(jvp())/conv_general_dilated | solution.py:97
  352.2 7.4 %reshape.967 = f32[36864]{0:T(1024)S(1)} reshape(f32[64,64,3,3]{3,2,1,0:T(4,128)} %copy.203) | data formatting | bytes 294912 | tf_op jit(solution)/shard_map/reshape | solution.py:743
  359.7 4.6 copy.202
  364.3 6.1 %reshape.966 = f32[32768]{0:T(1024)S(1)} reshape(f32[64,32,4,4]{3,2,1,0:T(4,128)} %copy.202) | data formatting | bytes 262144 | tf_op jit(solution)/shard_map/reshape | solution.py:743
  370.4 22.3 %fusion.222 = f32[32,4,8,8]{0,1,3,2:T(4,128)S(1)} fusion(bf16[120,4,84,84]{0,1,3,2:T(4,128)(2,1)} %copy.167, f32[120,32,20,20]{0,1,3,2:T(8,128)} %get-tuple-element.340), kind=kOutput, calls=%fused_computation.395 | convolution fusion | flops 2359296000 | bytes 12950528 | tf_op jit(solution)/shard_map/transpose(jvp())/conv_general_dilated | solution.py:97
  393.7 1.8 concatenate.23
  397.6 64.2 %conditional.1 = ((f32[8192,128]{1,0:T(8,128)}, f32[832,128]{1,0:T(8,128)}, f32[8,128]{1,0:T(8,128)S(1)})) conditional(s32[]{:T(128)} %convert_element_type.58, (s32[128]{0:T(128)S(1)}, s32[4]{0:T(128)S(1)}, s32[128]{0:T(128)S(1)}, s32[128]{0:T(128)S(1)}, f32[128,128]{1,0:T(8,128)S(1)}, /*index=5*/f32[3136,128]{1,0:T(8,128)S(1)}, ...), branch_computations={%region_62.64_spmd, %region_64.66_spmd} | conditional | flops 18432 | bytes 2099260 | solution.py:788
  401.3 1.8 slice.293.refs_2_
  403.1 58.7 %reduce_gradients.4 = (f32[8192,128]{1,0:T(8,128)}, f32[832,128]{1,0:T(8,128)}, f32[8,128]{1,0:T(8,128)S(1)}) custom-call(f32[3136,128]{1,0:T(8,128)S(1)} %get-tuple-element.107.refs_0_, f32[696,128]{1,0:T(8,128)} %get-tuple-element.108.refs_1_, f32[776,128]{1,0:T(8,128)} %slice.293.refs_2_, f32[776,128]{1,0:T(8,128)} %get-tuple-element.115.refs_3_, ...), custom_call_target="tpu_custom_call" | custom-call | tf_op jit(solution)/shard_map/cond/branch_1_fun/reduce_gradients/pallas_call | solution.py:410
  461.8 2.1 copy-done.1
  463.9 33.2 %adam_update.1 = (f32[7896,128]{1,0:T(8,128)}, f32[7896,128]{1,0:T(8,128)}, f32[7896,128]{1,0:T(8,128)}, f32[770,128]{1,0:T(8,128)}, f32[770,128]{1,0:T(8,128)},...) custom-call(s32[128]{0:T(128)S(1)} %reshape.938.starts_ref, s32[128]{0:T(128)S(1)} %reshape.939.lengths_ref, s32[1]{0:T(128)} %bitcast.8.flag_ref, ...), custom_call_target="tpu_custom_call" | custom-call | tf_op jit(solution)/shard_map/adam_update/pallas_call | solution.py:650
  497.1 3.7 bitcast_convert_fusion.1
  (501 shorter events, 99.9 us)
Async XLA Ops:
  7.2 166.3 %all-gather.4.cloned.1.call-start = ((), (), s32[]{:S(2)}) async-start(), calls=%async_computation | async-start | bytes 1971200 | tf_op jit(solution)/shard_map/all_gather | solution.py:713
  11.0 90.7 %copy-start.111 = (f32[128]{0:T(128)}, f32[128]{0:T(128)S(1)}, u32[]{:S(2)}) copy-start(f32[128]{0:T(128)S(1)} %get-tuple-element.282) | copy-start | bytes 1540
  11.0 90.7 %copy-start.113 = (f32[128]{0:T(128)}, f32[128]{0:T(128)S(1)}, u32[]{:S(2)}) copy-start(f32[128]{0:T(128)S(1)} %get-tuple-element.283) | copy-start | bytes 1540
  11.0 97.5 %copy-start.104 = (f32[128]{0:T(128)}, f32[128]{0:T(128)S(1)}, u32[]{:S(2)}) copy-start(f32[128]{0:T(128)S(1)} %get-tuple-element.280) | copy-start | bytes 1540
  11.0 187.7 %copy-start.98 = (f32[128]{0:T(128)}, f32[128]{0:T(128)S(1)}, u32[]{:S(2)}) copy-start(f32[128]{0:T(128)S(1)} %get-tuple-element.277) | copy-start | bytes 1540
  11.0 187.7 %copy-start.115 = (f32[128]{0:T(128)}, f32[128]{0:T(128)S(1)}, u32[]{:S(2)}) copy-start(f32[128]{0:T(128)S(1)} %get-tuple-element.276) | copy-start | bytes 1540
  11.0 189.2 %copy-start.106 = (f32[128]{0:T(128)}, f32[128]{0:T(128)S(1)}, u32[]{:S(2)}) copy-start(f32[128]{0:T(128)S(1)} %get-tuple-element.274) | copy-start | bytes 1540
  11.0 198.0 %copy-start.100 = (f32[128]{0:T(128)}, f32[128]{0:T(128)S(1)}, u32[]{:S(2)}) copy-start(f32[128]{0:T(128)S(1)} %get-tuple-element.271) | copy-start | bytes 1540
  11.0 201.4 %copy-start.108 = (f32[128]{0:T(128)}, f32[128]{0:T(128)S(1)}, u32[]{:S(2)}) copy-start(f32[128]{0:T(128)S(1)} %get-tuple-element.267) | copy-start | bytes 1540
  11.7 67.9 %copy-start.142 = (f32[32]{0:T(128)}, f32[32]{0:T(128)S(1)}, u32[]{:S(2)}) copy-start(f32[32]{0:T(128)S(1)} %slice.227) | copy-start | bytes 388
  13.5 73.0 %copy-start.140 = (f32[64]{0:T(128)}, f32[64]{0:T(128)S(1)}, u32[]{:S(2)}) copy-start(f32[64]{0:T(128)S(1)} %get-tuple-element.284) | copy-start | bytes 772
  18.5 21.8 %slice-start = ((f32[1010688]{0:T(1024)}), f32[8192]{0:T(1024)S(1)}, s32[]{:S(2)}) async-start(f32[1010688]{0:T(1024)} %param.18), calls=%async_computation.1 | async-start | bytes 65536 | tf_op jit(solution)/shard_map/slice | solution.py:52
  51.8 27.8 %copy-start.51 = (f32[64,32,4,4]{0,1,3,2:T(8,128)}, f32[64,32,4,4]{0,1,3,2:T(8,128)S(1)}, u32[]{:S(2)}) copy-start(f32[64,32,4,4]{0,1,3,2:T(8,128)S(1)} %copy.169) | copy-start | bytes 393220
  65.1 21.4 %copy-start.47 = (f32[64,64,3,3]{0,1,3,2:T(8,128)}, f32[64,64,3,3]{0,1,3,2:T(8,128)S(1)}, u32[]{:S(2)}) copy-start(f32[64,64,3,3]{0,1,3,2:T(8,128)S(1)} %copy.198) | copy-start | bytes 442372
  79.6 6.9 %copy-start.10 = (f32[120,32,20,20]{0,1,3,2:T(8,128)}, f32[120,32,20,20]{0,1,3,2:T(8,128)S(1)}, u32[]{:S(2)}) copy-start(f32[120,32,20,20]{0,1,3,2:T(8,128)S(1)} %fusion.221) | copy-start | bytes 18432004
  86.5 6.1 %copy-start.144 = (f32[120,64,9,9]{0,1,3,2:T(8,128)}, f32[120,64,9,9]{0,1,3,2:T(8,128)S(1)}, u32[]{:S(2)}) copy-start(f32[120,64,9,9]{0,1,3,2:T(8,128)S(1)} %fusion.70) | copy-start | bytes 7464964
  96.3 4.4 copy-start.76
  96.3 5.4 %copy-start.109 = (f32[4,30]{1,0:T(4,128)S(1)}, f32[4,30]{1,0:T(4,128)}, u32[]{:S(2)}) copy-start(f32[4,30]{1,0:T(4,128)} %param.14) | copy-start | bytes 1444
  100.6 4.4 copy-start.132
  101.7 7.2 %copy-start.33 = (f32[4,30,128]{2,1,0:T(8,128)}, f32[4,30,128]{2,1,0:T(8,128)S(1)}, u32[]{:S(2)}) copy-start(f32[4,30,128]{2,1,0:T(8,128)S(1)} %convolution_tanh_fusion) | copy-start | bytes 184324
  112.8 85.0 %copy-start.12 = (f32[360,128]{1,0:T(8,128)}, f32[360,128]{1,0:T(8,128)S(1)}, u32[]{:S(2)}) copy-start(f32[360,128]{1,0:T(8,128)S(1)} %add.522) | copy-start | bytes 552964
  171.2 9.0 %copy-start.66 = (s32[32,4]{1,0:T(8,128)}, s32[32,4]{1,0:T(8,128)S(1)}, u32[]{:S(2)}) copy-start(s32[32,4]{1,0:T(8,128)S(1)} %get-tuple-element.301) | copy-start | bytes 1540
  173.5 21.0 %copy-start.42 = (pred[4,90,90]{1,2,0:T(8,128)(4,1)}, pred[4,90,90]{1,2,0:T(8,128)(4,1)S(1)}, u32[]{:S(2)}) copy-start(pred[4,90,90]{1,2,0:T(8,128)(4,1)S(1)} %broadcast_and_fusion) | copy-start | bytes 97204
  188.6 9.2 %copy-start.38 = (f32[4,1,4096]{2,1,0:T(1,128)}, f32[4,1,4096]{2,1,0:T(1,128)S(1)}, u32[]{:S(2)}) copy-start(f32[4,1,4096]{2,1,0:T(1,128)S(1)} %get-tuple-element.295) | copy-start | bytes 196612
  207.9 4.2 copy-start.93
  210.5 5.5 %copy-start.37 = (f32[128,18]{1,0:T(8,128)S(1)}, f32[128,18]{1,0:T(8,128)}, u32[]{:S(2)}) copy-start(f32[128,18]{1,0:T(8,128)} %reshape.959) | copy-start | bytes 27652
  216.0 13.9 %copy-start.31 = (f32[4,30,1,128]{3,2,1,0:T(1,128)}, f32[4,30,1,128]{3,2,1,0:T(1,128)S(1)}, u32[]{:S(2)}) copy-start(f32[4,30,1,128]{3,2,1,0:T(1,128)S(1)} %slice.312) | copy-start | bytes 184324
  216.3 13.6 %copy-start.70 = (f32[4,30]{1,0:T(4,128)}, f32[4,30]{1,0:T(4,128)S(1)}, u32[]{:S(2)}) copy-start(f32[4,30]{1,0:T(4,128)S(1)} %get-tuple-element.331) | copy-start | bytes 1444
  220.8 9.0 %copy-start.35 = (f32[4,30,1,128]{3,1,0,2:T(8,128)}, f32[4,30,1,128]{3,1,0,2:T(8,128)S(1)}, u32[]{:S(2)}) copy-start(f32[4,30,1,128]{3,1,0,2:T(8,128)S(1)} %convolution_bitcast_fusion.13) | copy-start | bytes 184324
  223.4 6.5 %copy-start.30 = (f32[360,512]{1,0:T(8,128)S(1)}, f32[360,512]{1,0:T(8,128)}, u32[]{:S(2)}) copy-start(f32[360,512]{1,0:T(8,128)} %copy-done.29) | copy-start | bytes 2211844
  223.4 6.5 %copy-start.60 = (f32[4,1,16384]{2,1,0:T(1,128)S(1)}, f32[4,1,16384]{2,1,0:T(1,128)}, u32[]{:S(2)}) copy-start(f32[4,1,16384]{2,1,0:T(1,128)} %get-tuple-element.288) | copy-start | bytes 786436
  272.5 18.3 %slice-start.1 = ((s8[6553600]{0:T(1024)(128)(4,1)}), s8[4194304]{0:T(1024)(128)(4,1)S(1)}, s32[]{:S(2)}) async-start(s8[6553600]{0:T(1024)(128)(4,1)} %bitcast.350), calls=%async_computation.2 | async-start | bytes 8388608
  276.6 7.1 %copy-start.48 = (f32[64,64,3,3]{0,1,3,2:T(8,128)S(1)}, f32[64,64,3,3]{0,1,3,2:T(8,128)}, u32[]{:S(2)}) copy-start(f32[64,64,3,3]{0,1,3,2:T(8,128)} %copy-done.47) | copy-start | bytes 442372
  276.6 14.2 %slice-start.2 = ((s8[6553600]{0:T(1024)(128)(4,1)}), s8[2359296]{0:T(1024)(128)(4,1)S(1)}, s32[]{:S(2)}) async-start(s8[6553600]{0:T(1024)(128)(4,1)} %bitcast.350), calls=%async_computation.3 | async-start | bytes 4718592
  283.7 7.1 %copy-start.143 = (f32[32]{0:T(128)S(1)}, f32[32]{0:T(128)}, u32[]{:S(2)}) copy-start(f32[32]{0:T(128)} %copy-done.142) | copy-start | bytes 388
  290.8 10.3 %copy-start.52 = (f32[64,32,4,4]{0,1,3,2:T(8,128)S(1)}, f32[64,32,4,4]{0,1,3,2:T(8,128)}, u32[]{:S(2)}) copy-start(f32[64,32,4,4]{0,1,3,2:T(8,128)} %copy-done.51) | copy-start | bytes 393220
  323.6 4.2 copy-start.54
  323.6 4.3 copy-start.23
  352.2 7.4 %copy-start.53 = (f32[64,32,4,4]{0,1,3,2:T(8,128)S(1)}, f32[64,32,4,4]{0,1,3,2:T(8,128)}, u32[]{:S(2)}) copy-start(f32[64,32,4,4]{0,1,3,2:T(8,128)} %fusion.69) | copy-start | bytes 393220
  392.9 4.5 copy-start.138
  393.4 4.1 copy-start.5
  393.4 4.1 copy-start.67
  393.4 4.1 copy-start.103
  393.4 4.1 copy-start.133
  393.4 4.1 copy-start.134
  397.6 64.2 %copy-start.2 = (f32[98560]{0:T(1024)S(1)}, f32[98560]{0:T(1024)}, u32[]{:S(2)}) copy-start(f32[98560]{0:T(1024)} %param.21) | copy-start | bytes 1182724
  397.6 64.2 %copy-start.3 = (f32[98560]{0:T(1024)S(1)}, f32[98560]{0:T(1024)}, u32[]{:S(2)}) copy-start(f32[98560]{0:T(1024)} %param.22) | copy-start | bytes 1182724
  397.6 64.2 %copy-start.4 = (f32[98560]{0:T(1024)S(1)}, f32[98560]{0:T(1024)}, u32[]{:S(2)}) copy-start(f32[98560]{0:T(1024)} %param.23) | copy-start | bytes 1182724
  (102 other events, 231.1 us)
Sparse Core Ops, SparseCore 0:
  10.1 22.3 all-gather.3
